TPU v7x, 128 devices: a whole 4x4x4 slice. The times are simulated.
128 devices in a mesh: gx: 8 (over x, core), gy: 16 (over y, z).
Axes of the slice: x: 4, y: 4, z: 4, core: 2. Of those that a mesh axis runs over, the one named last changes fastest.
Arguments:
- features: bfloat16 [64, 1024, 2048], P(None, 'gx', 'gy'), may hold values from -6 to 6
- cotangent: bfloat16 [64, 1024, 2048], P(None, 'gx', 'gy'), may hold values from -6 to 6
- offsets: int32 [16, 2], replicated, may hold values from -2 to 2, as said below
- adjacency: int32 [64, 128, 8], replicated, may hold values from 0 to 8191, as said below
- near_weight: bfloat16 [16, 64, 64], replicated, may hold values from -0.1875 to 0.1875
- link_weight: bfloat16 [8, 64, 64], replicated, may hold values from -0.25 to 0.25
- top_weight: bfloat16 [64, 64], replicated, may hold values from -0.75 to 0.75
- top_kernel: float32 [128, 128], replicated, may hold values from -0.5 to 0.5
Outputs:
- output: bfloat16 [64, 1024, 2048], P(None, 'gx', 'gy')
- input_grad: bfloat16 [64, 1024, 2048], P(None, 'gx', 'gy')
- near_grad: float32 [16, 64, 64], replicated
- link_grad: float32 [8, 64, 64], replicated
- top_grad: float32 [64, 64], replicated
Inputs may be any that keep to these rules, and one draw needn't show every extreme that they name: `offsets`: each of the two columns takes both values -2 and 2 in some row. adjacency[i, j, l] names a level-1 cell at most 8 rows and at most 8 columns away from (i, j); row distance 8 and column distance 8 occur.
All inputs are finite; a program needn't handle non-finite values.
Results may differ from a plain program's by a relative error of at most 0.012.
Values may be sent and summed in bfloat16 or wider, within the bound.
A program may use at most 128 MiB of HBM per device.

v0:
```python
import jax
import jax.numpy as jnp
from jax import lax
from jax.sharding import PartitionSpec as P

OFFSETS = 16
RADIUS = 2
LINKS = 8
FACTOR = 16
FACTOR_TOP = 8


root_scale = 0.7978845608028654
cubic_term = 0.044715


def with_halo(block, sides, width):
    for axis, dim in sides:
        count = lax.axis_size(axis)
        forward = [(i, i + 1) for i in range(count - 1)]
        backward = [(target, source) for source, target in forward]
        low = lax.ppermute(
            lax.slice_in_dim(block, block.shape[dim] - width, None, axis=dim), axis, forward
        )
        high = lax.ppermute(lax.slice_in_dim(block, 0, width, axis=dim), axis, backward)
        block = jnp.concatenate([low, block, high], axis=dim)
    return block


def gelu_slope(values):
    inner_arg = root_scale * (values + cubic_term * values * values * values)
    tangent = jnp.tanh(inner_arg)
    return 0.5 * (1.0 + tangent) + 0.5 * values * (1.0 - tangent * tangent) * root_scale * (
        1.0 + 3.0 * cubic_term * values * values
    )


def pool_sum(values, factor):
    channels, height, breadth = values.shape
    return values.reshape(channels, height // factor, factor, breadth // factor, factor).sum(
        axis=(2, 4)
    )


def spread(values, factor):
    channels, height, breadth = values.shape
    widened = jnp.broadcast_to(
        values[:, :, None, :, None], (channels, height, factor, breadth, factor)
    )
    return widened.reshape(channels, height * factor, breadth * factor)


def window(padded, row_step, col_step, height, breadth):
    zero_index = jnp.zeros((), jnp.int32)
    starts = (zero_index, RADIUS + row_step, RADIUS + col_step)
    return lax.dynamic_slice(padded, starts, (padded.shape[0], height, breadth))


def to_grid(gathered, grid_rows, grid_cols, channels, height, breadth):
    shaped = gathered.reshape(grid_rows, grid_cols, channels, height, breadth)
    return shaped.transpose(2, 0, 3, 1, 4).reshape(
        channels, grid_rows * height, grid_cols * breadth
    )


def per_device(
    features, cotangent, offsets, adjacency, near_weight, link_weight, top_weight, top_kernel
):
    highest = lax.Precision.HIGHEST
    channels, height, breadth = features.shape
    grid_rows = lax.axis_size("gx")
    grid_cols = lax.axis_size("gy")
    coarse_rows = height // FACTOR
    coarse_cols = breadth // FACTOR
    top_rows = coarse_rows // FACTOR_TOP
    top_cols = coarse_cols // FACTOR_TOP
    total_coarse_cols = coarse_cols * grid_cols
    row_start = lax.axis_index("gx") * coarse_rows
    col_start = lax.axis_index("gy") * coarse_cols
    zero_index = jnp.zeros((), jnp.int32)
    border_rows = coarse_rows + 2 * coarse_cols
    border_cols = coarse_cols + 2 * coarse_cols
    padded = with_halo(features, (("gx", 1), ("gy", 2)), RADIUS)

    def near_step(offset_id, running):
        shifted = window(padded, offsets[offset_id, 0], offsets[offset_id, 1], height, breadth)
        return running + jnp.einsum(
            "cxy,cd->dxy", shifted, near_weight[offset_id], preferred_element_type=jnp.float32
        )

    near_field = lax.fori_loop(
        0, OFFSETS, near_step, jnp.zeros((channels, height, breadth), jnp.float32)
    )
    inputs_f32 = features.astype(jnp.float32)
    coarse = (pool_sum(inputs_f32, FACTOR) / FACTOR).astype(jnp.bfloat16)
    local_links = lax.dynamic_slice(
        adjacency, (row_start, col_start, zero_index), (coarse_rows, coarse_cols, LINKS)
    )
    gathered = lax.all_gather(coarse.reshape(1, -1), ("gx", "gy"), axis=0, tiled=True)
    coarse_grid = to_grid(gathered, grid_rows, grid_cols, channels, coarse_rows, coarse_cols)
    picked = coarse_grid.reshape(channels, -1)[:, local_links.reshape(-1)]
    top_coef = pool_sum(coarse_grid.astype(jnp.float32), FACTOR_TOP) / FACTOR_TOP
    picked = picked.reshape(channels, coarse_rows * coarse_cols, LINKS)
    level_one = jnp.einsum("cml,lcd->dm", picked, link_weight, preferred_element_type=jnp.float32)
    level_one = level_one.reshape(channels, coarse_rows, coarse_cols)
    total_top_rows = top_coef.shape[1]
    total_top_cols = top_coef.shape[2]
    top_flat = top_coef.reshape(channels, total_top_rows * total_top_cols)
    top_f32 = top_weight.astype(jnp.float32)
    mixed_top = jnp.einsum("cn,cd->dn", top_flat, top_f32, precision=highest)
    level_two = jnp.dot(mixed_top, top_kernel.T, precision=highest).reshape(
        channels, total_top_rows, total_top_cols
    )
    top_start = (zero_index, lax.axis_index("gx") * top_rows, lax.axis_index("gy") * top_cols)
    two_mine = lax.dynamic_slice(level_two, top_start, (channels, top_rows, top_cols))
    hidden = near_field + spread(level_one, FACTOR) + spread(two_mine, FACTOR * FACTOR_TOP)
    output = (inputs_f32 + jax.nn.gelu(hidden, approximate=True)).astype(jnp.bfloat16)
    upstream = cotangent.astype(jnp.float32)
    hidden_grad = (upstream * gelu_slope(hidden)).astype(jnp.bfloat16)

    def weight_step(offset_id, grads):
        shifted = window(padded, offsets[offset_id, 0], offsets[offset_id, 1], height, breadth)
        return grads.at[offset_id].set(
            jnp.einsum("cxy,dxy->cd", shifted, hidden_grad, preferred_element_type=jnp.float32)
        )

    near_part = lax.fori_loop(
        0, OFFSETS, weight_step, jnp.zeros((OFFSETS, channels, channels), jnp.float32)
    )
    grad_padded = with_halo(hidden_grad, (("gx", 1), ("gy", 2)), RADIUS)

    def back_step(offset_id, running):
        shifted = window(
            grad_padded, -offsets[offset_id, 0], -offsets[offset_id, 1], height, breadth
        )
        return running + jnp.einsum(
            "dxy,cd->cxy", shifted, near_weight[offset_id], preferred_element_type=jnp.float32
        )

    back_near = lax.fori_loop(
        0, OFFSETS, back_step, jnp.zeros((channels, height, breadth), jnp.float32)
    )
    grad_f32 = hidden_grad.astype(jnp.float32)
    one_flat = pool_sum(grad_f32, FACTOR).reshape(channels, coarse_rows * coarse_cols)
    two_grad = pool_sum(grad_f32, FACTOR * FACTOR_TOP)
    link_f32 = link_weight.astype(jnp.float32)
    link_part = jnp.einsum("cml,dm->lcd", picked.astype(jnp.float32), one_flat, precision=highest)
    one_grid = one_flat.reshape(channels, coarse_rows, coarse_cols)
    near_grads = with_halo(one_grid, (("gx", 1), ("gy", 2)), coarse_cols)
    links_wide = jnp.pad(
        adjacency, ((coarse_cols, coarse_cols), (coarse_cols, coarse_cols), (0, 0))
    )
    near_links = lax.dynamic_slice(
        links_wide, (row_start, col_start, zero_index), (border_rows, border_cols, LINKS)
    )
    near_pushed = jnp.einsum(
        "dm,lcd->cml", near_grads.reshape(channels, -1), link_f32, precision=highest
    ).reshape(channels, -1)
    every_rows = near_links // total_coarse_cols
    every_cols = near_links % total_coarse_cols
    inside = (every_rows >= row_start) & (every_rows < row_start + coarse_rows)
    inside = inside & (every_cols >= col_start) & (every_cols < col_start + coarse_cols)
    own_cells = coarse_rows * coarse_cols
    target_slot = jnp.where(
        inside, (every_rows - row_start) * coarse_cols + (every_cols - col_start), own_cells
    )
    collected = (
        jnp.zeros((channels, own_cells + 1), jnp.float32)
        .at[:, target_slot.reshape(-1)]
        .add(near_pushed)
    )
    coarse_grad = collected[:, :own_cells].reshape(channels, coarse_rows, coarse_cols)
    top_grads = lax.all_gather(two_grad.reshape(1, -1), ("gx", "gy"), axis=0, tiled=True)
    two_all = to_grid(top_grads, grid_rows, grid_cols, channels, top_rows, top_cols).reshape(
        channels, -1
    )
    kernel_grad = jnp.dot(two_all, top_kernel, precision=highest)
    top_grad = jnp.einsum("cn,dn->cd", top_flat, kernel_grad, precision=highest)
    top_coef_grad = jnp.einsum("dn,cd->cn", kernel_grad, top_f32, precision=highest)
    top_coef_grad = top_coef_grad.reshape(channels, total_top_rows, total_top_cols)
    coef_mine = lax.dynamic_slice(top_coef_grad, top_start, (channels, top_rows, top_cols))
    coarse_grad = coarse_grad + spread(coef_mine, FACTOR_TOP) / FACTOR_TOP
    weight_total = lax.psum((near_part, link_part), ("gx", "gy"))
    input_grad = upstream + back_near + spread(coarse_grad, FACTOR) / FACTOR
    return (output, input_grad.astype(jnp.bfloat16), weight_total[0], weight_total[1], top_grad)


def solution(mesh):
    placed = (P(None, "gx", "gy"), P(None, "gx", "gy"), P(), P(), P(), P(), P(), P())
    return jax.shard_map(
        per_device,
        mesh=mesh,
        in_specs=placed,
        out_specs=(P(None, "gx", "gy"), P(None, "gx", "gy"), P(), P(), P()),
        check_vma=False,
    )
```

profile of v0, /device:TPU:1, one launch (start us, length us, event | category | flops | bytes accessed | tf_op | source)
XLA Modules:
  0.0 727.4 jit_solution(4743669426479916425)
XLA Ops:
  7.2 5.4 copy.112
  17.8 4.5 collective-permute-start
  28.4 4.2 copy.115
  32.6 4.2 copy.117
  42.8 5.4 copy.128
  48.2 5.7 pad_maximum_fusion.1
  53.9 9.3 %copy.119 = bf16[64,132,132]{2,0,1:T(8,128)(2,1)} copy(bf16[64,132,132]{1,0,2:T(8,128)(2,1)} %pad_maximum_fusion.1) | data formatting | bytes 4460544
  63.2 155.4 %while.52 = (s32[]{:T(128)}, f32[64,128,128]{2,0,1:T(8,128)}, bf16[16,64,64]{2,1,0:T(8,128)(2,1)}, s32[16,2]{0,1:T(2,128)S(1)}, bf16[64,132,132]{2,0,1:T(8,128)(...) while((s32[]{:T(128)}, f32[64,128,128]{2,0,1:T(8,128)}, ...), condition=%wide.region_1.0_spmd.clone, body=%wide.region_0.0_spmd.clone.sunk | while | flops 136314896 | bytes 10502879 | solution.py:91
  66.4 5.3 select_add_fusion.4
  74.9 6.7 select_add_fusion.4
  84.8 6.6 select_add_fusion.4
  94.6 6.6 select_add_fusion.4
  104.3 6.6 select_add_fusion.4
  114.1 6.6 select_add_fusion.4
  123.9 6.6 select_add_fusion.4
  133.7 6.6 select_add_fusion.4
  143.5 6.6 select_add_fusion.4
  153.3 6.6 select_add_fusion.4
  163.1 6.6 select_add_fusion.4
  172.9 6.6 select_add_fusion.4
  182.7 6.6 select_add_fusion.4
  192.4 6.6 select_add_fusion.4
  202.2 6.6 select_add_fusion.4
  212.0 6.6 select_add_fusion.4
  218.6 6.9 copy.125
  225.5 5.0 copy.121
  230.6 7.4 %reshape.255 = bf16[8,16,64,8,8]{1,0,4,3,2:T(8,128)(2,1)} reshape(bf16[128,1,4096]{0,2,1:T(8,128)(2,1)S(1)} %copy.121) | data formatting | bytes 2097152 | tf_op jit(solution)/shard_map/reshape | solution.py:60
  238.0 5.6 convert_reduce_fusion
  243.7 11.8 %copy.122 = bf16[64,8,8,16,8]{0,4,3,2,1:T(8,128)(2,1)S(1)} copy(bf16[64,8,8,16,8]{3,1,4,2,0:T(8,128)(2,1)} %bitcast.136) | data formatting | bytes 2097152 | tf_op jit(solution)/shard_map/transpose | solution.py:61
  260.8 13.0 %convert_reduce_fusion.1 = (f32[64]{0:T(128)S(1)}, bf16[64,128,128]{0,2,1:T(8,128)(2,1)}, bf16[64,128,128]{0,2,1:T(8,128)(2,1)}) fusion(f32[64]{0:T(128)S(1)} %fusion.45, f32[64,128,128]{0,2,1:T(8,128)} %copy.125, f32[64,128,128]{0,2,1:T(8,128)S(1)} %bitcast.138, bf16[64,128,128]{0,2,1:T(8,128)(2,1)S(1)} %copy-done.2, bf16[64,128,128]{0,2,1:T(8,128)(2,1)S(1)} %copy-done.1), kind=kLoop, calls=%fused_computation.53 | loop fusion | flops 36700096 | bytes 16777728 | tf_op jit(solution)/shard_map/reduce_sum | solution.py:40
  282.7 3.9 collective-permute-start.8
  288.9 68.0 %all-reduce.1 = f32[8192]{0:T(1024)S(1)} all-reduce(f32[8192]{0:T(1024)S(1)} %dynamic-update-slice.11), channel_id=2, replica_groups=mesh['gx'=8,'gy'=16] {'gx','gy'}, use_global_device_ids=true, to_apply=%add.1 | all-reduce | flops 8192 | bytes 65536
  358.3 123.8 %while.51 = (s32[]{:T(128)}, f32[16,64,64]{2,1,0:T(8,128)S(1)}, s32[16,2]{0,1:T(2,128)S(1)}, bf16[64,132,132]{2,0,1:T(8,128)(2,1)}, bf16[64,128,128]{2,0,1:T(8,1...) while((s32[]{:T(128)}, f32[16,64,64]{2,1,0:T(8,128)S(1)}, ...), condition=%wide.region_11.12_spmd, body=%wide.region_9.11_spmd.sunk | while | flops 134221856 | bytes 4261114 | solution.py:127
  362.2 3.8 fusion.80
  370.0 3.8 fusion.80
  377.7 3.8 fusion.80
  400.9 3.8 fusion.80
  462.8 3.8 fusion.80
  487.5 5.6 copy.139
  497.8 4.0 collective-permute-start.6
  507.2 29.1 %scatter_custom_fusion = f32[64,65]{0,1:T(8,128)S(1)} fusion(s32[4608]{0:T(1024)S(1)} %fusion.43, f32[64,576,8]{0,2,1:T(8,128)S(1)} %copy.133, f32[]{:T(128)} %constant.297.clone.1), kind=kCustom, calls=%fused_computation.51 | custom fusion | flops 294912 | bytes 2375940 | tf_op jit(solution)/shard_map/scatter-add | solution.py:170
  536.4 8.9 %pad_maximum_fusion = bf16[64,132,132]{0,2,1:T(8,128)(2,1)} fusion(bf16[64,132,2]{0,2,1:T(2,128)(2,1)S(1)} %collective-permute-done.7, bf16[64,2,128]{0,2,1:T(8,128)(2,1)S(1)} %collective-permute-done.5, bf16[64,128,128]{0,2,1:T(8,128)(2,1)} %get-tuple-element.643, bf16[64,2,128]{0,2,1:T(8,128)(2,1)S(1)} %collective-permute-done.4, ...), kind=kLoop, calls=%fused_computation.49 | loop fusion | flops 11151360 | bytes 4460544 | tf_op jit(solution)/shard_map/concatenate | solution.py:26
  545.3 6.9 copy.129
  552.2 136.6 %while.53 = (s32[]{:T(128)}, f32[64,128,128]{2,0,1:T(8,128)}, bf16[16,64,64]{2,1,0:T(8,128)(2,1)}, s32[16,2]{0,1:T(2,128)S(1)}, bf16[64,132,132]{2,0,1:T(8,128)(...) while((s32[]{:T(128)}, f32[64,128,128]{2,0,1:T(8,128)}, ...), condition=%wide.region_5.6_spmd.clone, body=%wide.region_4.5_spmd.clone.sunk | while | flops 136314896 | bytes 10502895 | solution.py:140
  554.2 5.3 select_add_fusion.5
  561.5 6.6 select_add_fusion.5
  570.1 6.6 select_add_fusion.5
  578.8 6.6 select_add_fusion.5
  587.4 6.6 select_add_fusion.5
  596.0 6.6 select_add_fusion.5
  604.6 6.6 select_add_fusion.5
  613.2 6.6 select_add_fusion.5
  621.9 6.6 select_add_fusion.5
  630.5 6.6 select_add_fusion.5
  639.1 6.6 select_add_fusion.5
  647.8 6.6 select_add_fusion.5
  656.4 6.6 select_add_fusion.5
  665.0 6.6 select_add_fusion.5
  673.6 6.6 select_add_fusion.5
  682.2 6.6 select_add_fusion.5
  688.8 6.9 copy.130
  695.7 4.2 broadcast_in_dim.43
  699.9 11.4 %fusion.22 = bf16[64,128,128]{0,2,1:T(8,128)(2,1)} fusion(f32[64,128,128]{0,2,1:T(8,128)} %bitcast.139, f32[64,128,128]{0,2,1:T(8,128)} %copy.130, bf16[64,128,128]{0,2,1:T(8,128)(2,1)} %copy.128), kind=kLoop, calls=%fused_computation.33 | loop fusion | flops 4194304 | bytes 12582912 | tf_op jit(solution)/shard_map/convert_element_type | solution.py:185
  711.3 5.6 copy.140
  (170 shorter events, 136.6 us)
Async XLA Ops:
  7.2 250.0 %copy-start = (bf16[8,64,64]{2,1,0:T(8,128)(2,1)S(1)}, bf16[8,64,64]{2,1,0:T(8,128)(2,1)}, u32[]{:S(2)}) copy-start(bf16[8,64,64]{2,1,0:T(8,128)(2,1)} %param.21) | copy-start | bytes 196612
  7.2 17.1 %copy-start.4 = (s32[64,128,8]{1,2,0:T(8,128)S(1)}, s32[64,128,8]{1,2,0:T(8,128)}, u32[]{:S(2)}) copy-start(s32[64,128,8]{1,2,0:T(8,128)} %param.19) | copy-start | bytes 786436
  7.2 218.3 %all-gather.4.cloned.1.call-start = ((), (), s32[]{:S(2)}) async-start(), calls=%async_computation | async-start | bytes 2113536 | tf_op jit(solution)/shard_map/all_gather | solution.py:99
  16.7 700.2 %all-reduce.5.cloned.1.call-start = ((), (), s32[]{:S(2)}) async-start(), calls=%async_computation.1 | async-start | bytes 1572864 | tf_op jit(solution)/shard_map/psum | solution.py:183
  17.8 10.7 %collective-permute-start = (bf16[64,2,128]{2,0,1:T(8,128)(2,1)S(1)}, bf16[64,2,128]{2,0,1:T(8,128)(2,1)S(1)}, u32[]{:S(2)}, u32[]{:S(2)}) collective-permute-start(bf16[64,2,128]{2,0,1:T(8,128)(2,1)S(1)} %copy.148), channel_id=1, source_target_pairs={{0,16},{16,32},{32,48},{48,64},{64,80},{80,96},{96,112},{1,17},{17... | collective-permute-start | bytes 98312 | tf_op jit(solution)/shard_map/ppermute | solution.py:22
  22.3 10.3 %collective-permute-start.1 = (bf16[64,2,128]{2,0,1:T(8,128)(2,1)S(1)}, bf16[64,2,128]{2,0,1:T(8,128)(2,1)S(1)}, u32[]{:S(2)}, u32[]{:S(2)}) collective-permute-start(bf16[64,2,128]{2,0,1:T(8,128)(2,1)S(1)} %copy.149), channel_id=1, source_target_pairs={{16,0},{32,16},{48,32},{64,48},{80,64},{96,80},{112,96},{17,1},{33... | collective-permute-start | bytes 98312 | tf_op jit(solution)/shard_map/ppermute | solution.py:25
  37.7 10.4 %collective-permute-start.2 = (bf16[64,132,2]{1,0,2:T(8,128)(2,1)S(1)}, bf16[64,132,2]{1,0,2:T(8,128)(2,1)S(1)}, u32[]{:S(2)}, u32[]{:S(2)}) collective-permute-start(bf16[64,132,2]{1,0,2:T(8,128)(2,1)S(1)} %get-tuple-element.651), channel_id=1, source_target_pairs={{0,1},{1,2},{2,3},{3,4},{4,5},{5,6},{6,7},{7,8},{8,9},{9,10},{10,1... | collective-permute-start | bytes 101384 | tf_op jit(solution)/shard_map/ppermute | solution.py:22
  41.3 6.9 collective-permute-start.3
  53.9 9.3 %copy-start.6 = (s32[16,2]{0,1:T(2,128)S(1)}, s32[16,2]{0,1:T(2,128)}, u32[]{:S(2)}) copy-start(s32[16,2]{0,1:T(2,128)} %param.18) | copy-start | bytes 388
  243.7 13.7 %copy-start.7 = (bf16[64,64]{1,0:T(8,128)(2,1)S(1)}, bf16[64,64]{1,0:T(8,128)(2,1)}, u32[]{:S(2)}) copy-start(bf16[64,64]{1,0:T(8,128)(2,1)} %param.22) | copy-start | bytes 24580
  243.7 13.9 %copy-start.5 = (f32[128,128]{1,0:T(8,128)S(1)}, f32[128,128]{1,0:T(8,128)}, u32[]{:S(2)}) copy-start(f32[128,128]{1,0:T(8,128)} %param.23) | copy-start | bytes 196612
  257.4 2.2 copy-start.1
  257.4 3.5 copy-start.2
  277.5 80.8 %copy-start.8 = (s32[3]{0:T(128)S(1)}, s32[3]{0:T(128)}, u32[]{:S(2)}) copy-start(s32[3]{0:T(128)} %constant.291.clone.1) | copy-start | bytes 40
  282.7 210.4 %collective-permute-start.8 = (f32[64,8,8]{0,2,1:T(8,128)S(1)}, f32[64,8,8]{0,2,1:T(8,128)S(1)}, u32[]{:S(2)}, u32[]{:S(2)}) collective-permute-start(f32[64,8,8]{0,2,1:T(8,128)S(1)} %reduce_sum.38), channel_id=1, source_target_pairs={{0,16},{16,32},{32,48},{48,64},{64,80},{80,96},{96,112},{1,17},{17... | collective-permute-start | bytes 49160 | tf_op jit(solution)/shard_map/ppermute | solution.py:22
  286.7 206.5 %collective-permute-start.9 = (f32[64,8,8]{0,2,1:T(8,128)S(1)}, f32[64,8,8]{0,2,1:T(8,128)S(1)}, u32[]{:S(2)}, u32[]{:S(2)}) collective-permute-start(f32[64,8,8]{0,2,1:T(8,128)S(1)} %reduce_sum.38), channel_id=1, source_target_pairs={{16,0},{32,16},{48,32},{64,48},{80,64},{96,80},{112,96},{17,1},{33... | collective-permute-start | bytes 49160 | tf_op jit(solution)/shard_map/ppermute | solution.py:25
  482.1 11.0 %copy-start.3 = (f32[16,64,64]{2,1,0:T(8,128)}, f32[16,64,64]{2,1,0:T(8,128)S(1)}, u32[]{:S(2)}) copy-start(f32[16,64,64]{2,1,0:T(8,128)S(1)} %get-tuple-element.473) | copy-start | bytes 786436
  482.1 14.5 %collective-permute-start.4 = (bf16[64,2,128]{0,2,1:T(8,128)(2,1)S(1)}, bf16[64,2,128]{0,2,1:T(8,128)(2,1)S(1)}, u32[]{:S(2)}, u32[]{:S(2)}) collective-permute-start(bf16[64,2,128]{0,2,1:T(8,128)(2,1)S(1)} %get-tuple-element.655), channel_id=1, source_target_pairs={{0,16},{16,32},{32,48},{48,64},{64,80},{80,96},{96,112},{1,17},{17... | collective-permute-start | bytes 98312 | tf_op jit(solution)/shard_map/ppermute | solution.py:22
  485.5 11.2 %collective-permute-start.5 = (bf16[64,2,128]{0,2,1:T(8,128)(2,1)S(1)}, bf16[64,2,128]{0,2,1:T(8,128)(2,1)S(1)}, u32[]{:S(2)}, u32[]{:S(2)}) collective-permute-start(bf16[64,2,128]{0,2,1:T(8,128)(2,1)S(1)} %get-tuple-element.656), channel_id=1, source_target_pairs={{16,0},{32,16},{48,32},{64,48},{80,64},{96,80},{112,96},{17,1},{33... | collective-permute-start | bytes 98312 | tf_op jit(solution)/shard_map/ppermute | solution.py:25
  493.2 10.0 %collective-permute-start.10 = (f32[64,24,8]{0,2,1:T(8,128)S(1)}, f32[64,24,8]{0,2,1:T(8,128)S(1)}, u32[]{:S(2)}, u32[]{:S(2)}) collective-permute-start(f32[64,24,8]{0,2,1:T(8,128)S(1)} %pad_maximum_fusion.3), channel_id=1, source_target_pairs={{0,1},{1,2},{2,3},{3,4},{4,5},{5,6},{6,7},{7,8},{8,9},{9,10},{10,1... | collective-permute-start | bytes 147464 | tf_op jit(solution)/shard_map/ppermute | solution.py:22
  495.3 7.8 %collective-permute-start.11 = (f32[64,24,8]{0,2,1:T(8,128)S(1)}, f32[64,24,8]{0,2,1:T(8,128)S(1)}, u32[]{:S(2)}, u32[]{:S(2)}) collective-permute-start(f32[64,24,8]{0,2,1:T(8,128)S(1)} %pad_maximum_fusion.3), channel_id=1, source_target_pairs={{1,0},{2,1},{3,2},{4,3},{5,4},{6,5},{7,6},{8,7},{9,8},{10,9},{11,1... | collective-permute-start | bytes 147464 | tf_op jit(solution)/shard_map/ppermute | solution.py:25
  497.8 38.5 %collective-permute-start.6 = (bf16[64,132,2]{0,2,1:T(2,128)(2,1)S(1)}, bf16[64,132,2]{0,2,1:T(2,128)(2,1)S(1)}, u32[]{:S(2)}, u32[]{:S(2)}) collective-permute-start(bf16[64,132,2]{0,2,1:T(2,128)(2,1)S(1)} %get-tuple-element.653), channel_id=1, source_target_pairs={{0,1},{1,2},{2,3},{3,4},{4,5},{5,6},{6,7},{7,8},{8,9},{9,10},{10,1... | collective-permute-start | bytes 101384 | tf_op jit(solution)/shard_map/ppermute | solution.py:22
  501.8 34.5 %collective-permute-start.7 = (bf16[64,132,2]{0,2,1:T(2,128)(2,1)S(1)}, bf16[64,132,2]{0,2,1:T(2,128)(2,1)S(1)}, u32[]{:S(2)}, u32[]{:S(2)}) collective-permute-start(bf16[64,132,2]{0,2,1:T(2,128)(2,1)S(1)} %get-tuple-element.654), channel_id=1, source_target_pairs={{1,0},{2,1},{3,2},{4,3},{5,4},{6,5},{7,6},{8,7},{9,8},{10,9},{11,1... | collective-permute-start | bytes 101384 | tf_op jit(solution)/shard_map/ppermute | solution.py:25
Sparse Core Ops, SparseCore 0:
  16.8 68.8 all-gather.3
  493.3 144.3 all-reduce.4
where the time goes:
time: 737 us; the launch traced here: 727 us
  matrix products  275 us (37%)
  local copies, waits for them, and re-layouts  140 us (19%)
  loops' own time  105 us (14%)
  other arithmetic  93.8 us (13%)
  blocking collectives  68 us (9%)
  starting transfers between devices  31.3 us (4%)
  between operations  14.6 us (2%)
    dot_general x16, matrix products, near_step(): jnp.einsum('cxy,cd->dxy', shifted, near_weight[offset_id], preferred_elem...  104 us
    dot_general x16, matrix products, back_step(): jnp.einsum('dxy,cd->cxy', shifted, near_weight[offset_id], preferred_elem...  104 us
    unnamed x1, blocking collectives  68 us
    dot_general x16, matrix products, weight_step(): jnp.einsum('cxy,dxy->cd', shifted, hidden_grad, preferred_element_type=jn...  61 us
    unnamed x32, local copies, waits for them, and re-layouts  48.3 us
    another operation x1, loops' own time, per_device(): lax.fori_loop(0, OFFSETS, weight_step, jnp.zeros((OFFSETS, channels, chan...  42 us
    another operation x1, loops' own time, per_device(): lax.fori_loop(0, OFFSETS, near_step, jnp.zeros((channels, height, breadth...  41.6 us
    scatter-add x1, other arithmetic, per_device(): collected = jnp.zeros((channels, own_cells + 1), jnp.float32).at[:, targe...  29.1 us
  transfers between devices with their start and end apart: 14, of which 0 were waited for; matrix products, arithmetic and copies ran while one was open for 60% of the time, Pallas kernels for 0%

commit v1 on v0

v1 whole, which is shorter than its diff:
```python
import functools

import jax
import jax.numpy as jnp
from jax import lax
from jax.experimental import pallas as pl
from jax.experimental.pallas import tpu as pltpu
from jax.sharding import PartitionSpec as P

C = 64
N = 128
K = 16
L = 8
CELL = 16
B = 8
W = 5
R = 2
HALO = N + 2 * R
GROUP = 4
BAND = GROUP + 2 * R
TARGETS = 640

root_scale = 0.7978845608028654
cubic_term = 0.044715

bf16 = jnp.bfloat16
f32 = jnp.float32
MESH = pl.DeviceIdType.MESH
HIGHEST = lax.Precision.HIGHEST
NT = (((1,), (1,)), ((), ()))
NN = (((1,), (0,)), ((), ()))
TN = (((0,), (0,)), ((), ()))


def dot(a, b, dims=NN, precision=None):
    return lax.dot_general(a, b, dims, preferred_element_type=f32, precision=precision)


def split_dot(a, b, dims=NN, terms=3):
    total = None
    for _ in range(terms):
        high = a.astype(bf16)
        part = dot(high, b, dims)
        total = part if total is None else total + part
        a = a - high.astype(f32)
    return total


def dot_split(a, b, dims=NN, terms=2):
    total = None
    for _ in range(terms):
        high = b.astype(bf16)
        part = dot(a, high, dims)
        total = part if total is None else total + part
        b = b - high.astype(f32)
    return total


def kernel(
    nx, ny,
    feat, cot, adj, offs, nw, lw, tw, tk,
    out, ingrad, near_out, link_out, top_out,
    fbuf, cbuf, abuf, xs, hs, xpack, hpack, xright, xleft, hright, hleft,
    wide, wide_t, w5, w5t, fwd, bwd, spread, pooled, onehot, idx,
    coarse_nb, picked, base, top1, top2, two1, two2, ctr, rctr, grads,
    rs_src, rs1, rs2_src, rs2, ag1, ag2, obuf, ibuf, one_ref, codes, code_pairs,
    load_sem, store_sem, halo_s, halo_r, hhalo_s, hhalo_r, co_s, co_r, ct_s, ct_r,
    t1_s, t1_r, t2_s, t2_r, u1_s, u1_r, u2_s, u2_r,
    r1_s, r1_r, r2_s, r2_r, a1_s, a1_r, a2_s, a2_r,
):
    gx = lax.axis_index("gx")
    gy = lax.axis_index("gy")

    def at(dx, dy):
        return (lax.rem(gx + dx + nx, nx), lax.rem(gy + dy + ny, ny))

    loads = [
        pltpu.make_async_copy(feat, fbuf, load_sem.at[0]),
        pltpu.make_async_copy(cot, cbuf, load_sem.at[1]),
        pltpu.make_async_copy(adj.at[pl.ds(gx * B, B)], abuf, load_sem.at[2]),
    ]
    for load in loads:
        load.start()

    barrier = pltpu.get_barrier_semaphore()
    for j in range(1, nx):
        pl.semaphore_signal(barrier, inc=1, device_id=at(j, 0), device_id_type=MESH)
    for j in range(1, ny):
        pl.semaphore_signal(barrier, inc=1, device_id=at(0, j), device_id_type=MESH)
    for dx in (-1, 1):
        for dy in (-1, 1):
            pl.semaphore_signal(barrier, inc=1, device_id=at(dx, dy), device_id_type=MESH)

    lane = lax.broadcasted_iota(jnp.int32, (C, N), 1)
    low = lane < C

    def build_spread(i, carry):
        rows = lax.broadcasted_iota(jnp.int32, (N, N), 0) % C
        cols = lax.broadcasted_iota(jnp.int32, (N, N), 1) // CELL + i * B
        hit = jnp.where(rows == cols, 1.0, 0.0).astype(bf16)
        spread[:, pl.ds(pl.multiple_of(i * N, N), N)] = hit
        return carry

    lax.fori_loop(0, B, build_spread, 0)
    xpack[...] = jnp.zeros_like(xpack)
    rs_src[...] = jnp.zeros_like(rs_src)
    hpack[...] = jnp.zeros_like(hpack)

    def pack_edges(block, i, pack):
        first = jnp.zeros((C, N), bf16)
        last = jnp.zeros((C, N), bf16)
        for x in range(CELL):
            turned = pltpu.roll(block[x], 2 * x, 1) if x else block[x]
            first = jnp.where((lane >= 2 * x) & (lane < 2 * x + 2), turned, first)
            spot = (2 * x - 2) % N
            last = jnp.where((lane >= spot) & (lane < spot + 2), turned, last)
        shift = 2 * CELL * lax.rem(i, 4) + 2
        half = i // 4
        pack[0, half] = pack[0, half] + pltpu.roll(first, shift, 1)
        pack[1, half] = pack[1, half] + pltpu.roll(last, shift, 1)

    loads[0].wait()

    def arrange(i, carry):
        block = jnp.swapaxes(fbuf[:, pl.ds(pl.multiple_of(i * CELL, CELL), CELL), :], 0, 1)
        xs[R, pl.ds(R + i * CELL, CELL)] = block
        total = block[0].astype(f32)
        for x in range(1, CELL):
            total = total + block[x].astype(f32)
        pooled[:, pl.ds(pl.multiple_of(i * N, N), N)] = total
        pack_edges(block, i, xpack)
        return carry

    lax.fori_loop(0, B, arrange, 0)

    def halo_copies(field, pack, right, left, send, recv):
        mid = field.at[R]
        plan = [
            (mid.at[pl.ds(R, R)], mid.at[pl.ds(R + N, R)], (-1, 0)),
            (mid.at[pl.ds(N, R)], mid.at[pl.ds(0, R)], (1, 0)),
            (pack.at[0], right.at[pl.ds(1, 2)], (0, -1)),
            (pack.at[1], left.at[pl.ds(1, 2)], (0, 1)),
            (pack.at[0, 0], right.at[3], (-1, -1)),
            (pack.at[0, 1], right.at[0], (1, -1)),
            (pack.at[1, 0], left.at[3], (-1, 1)),
            (pack.at[1, 1], left.at[0], (1, 1)),
        ]
        return [
            pltpu.make_async_remote_copy(
                src_ref=src, dst_ref=dst, send_sem=send.at[n], recv_sem=recv.at[n],
                device_id=at(*way), device_id_type=MESH,
            )
            for n, (src, dst, way) in enumerate(plan)
        ]

    def finish_halo(field, right, left):
        up, down = gx > 0, gx < nx - 1
        field[R, pl.ds(0, R)] = jnp.where(up, field[R, pl.ds(0, R)], jnp.zeros((R, C, N), bf16))
        field[R, pl.ds(R + N, R)] = jnp.where(
            down, field[R, pl.ds(R + N, R)], jnp.zeros((R, C, N), bf16)
        )
        for side, inside in ((right, gy < ny - 1), (left, gy > 0)):
            for part, there in ((0, inside & up), (1, inside), (2, inside), (3, inside & down)):
                side[part] = jnp.where(there, side[part], jnp.zeros((C, N), bf16))

        def shift(step, carry):
            for n in range(4):
                t = step * 4 + n
                place = t + (C - R)
                part = place // C
                s = 2 * lax.rem(place, C) + 2
                mixed = jnp.where(((lane - (s - 2)) & (N - 1)) < 2, left[part], right[part])
                edge = pltpu.roll(mixed, lax.rem(2 * N - s, N), 1)
                slab = field[R, t]
                field[0, t] = pltpu.roll(jnp.where(lane >= N - 2, edge, slab), 2, 1)
                field[1, t] = pltpu.roll(jnp.where(lane >= N - 1, edge, slab), 1, 1)
                field[3, t] = pltpu.roll(jnp.where(lane < 1, edge, slab), N - 1, 1)
                field[4, t] = pltpu.roll(jnp.where(lane < 2, edge, slab), N - 2, 1)
            return carry

        lax.fori_loop(0, HALO // 4, shift, 0)

    def around():
        return [(dx, dy) for dx in (-1, 0, 1) for dy in (-1, 0, 1) if (dx, dy) != (0, 0)]

    def line(axis, src, dst, send, recv):
        n = nx if axis == "gx" else ny
        me = gx if axis == "gx" else gy

        def copy(j, source, target):
            peer = lax.rem(me + j, n)
            return pltpu.make_async_remote_copy(
                src_ref=src(source(peer)), dst_ref=dst(target), send_sem=send.at[j],
                recv_sem=recv.at[j],
                device_id=(peer, gy) if axis == "gx" else (gx, peer), device_id_type=MESH,
            )

        def start():
            def step(j, carry):
                copy(j, lambda peer: peer, me).start()
                return carry

            lax.fori_loop(1, n, step, 0)

        def wait():
            def step(j, carry):
                copy(j, lambda peer: peer, lax.rem(me + n - j, n)).wait_recv()
                copy(j, lambda peer: peer, me).wait_send()
                return carry

            lax.fori_loop(1, n, step, 0)

        return start, wait

    pl.semaphore_wait(barrier, nx - 1 + ny - 1 + 4)
    xhalo = halo_copies(xs, xpack, xright, xleft, halo_s, halo_r)
    for copy in xhalo:
        copy.start()

    coarse = (split_dot(pooled[...], spread[...], NT) / CELL).astype(bf16)
    coarse_nb[4] = coarse
    coarse_copies = []
    for n, (dx, dy) in enumerate(around()):
        slot = (1 - dx) * 3 + (1 - dy)
        copy = pltpu.make_async_remote_copy(
            src_ref=coarse_nb.at[4], dst_ref=coarse_nb.at[slot], send_sem=co_s.at[n],
            recv_sem=co_r.at[n], device_id=at(dx, dy), device_id_type=MESH,
        )
        copy.start()
        coarse_copies.append(copy)
    ones = jnp.where(lax.broadcasted_iota(jnp.int32, (8, N), 1) < C, 1.0, 0.0)

    def as_row(values):
        sums = dot(ones, values, NT, HIGHEST)
        return jnp.concatenate([sums, jnp.zeros((8, N - C), f32)], axis=1)

    top1[gy] = as_row(coarse.astype(f32)) / B
    t1_start, t1_wait = line("gy", lambda p: top1.at[gy], lambda p: top1.at[p], t1_s, t1_r)
    t1_start()

    def widen(k, carry):
        block = nw[k].astype(f32)
        wide[k] = jnp.concatenate([block, block], axis=1)
        turned = block.T
        wide_t[k] = jnp.concatenate([turned, turned], axis=1)
        return carry

    lax.fori_loop(0, K, widen, 0)

    code = (offs[pl.ds(0, 1), :] + R) * W + offs[pl.ds(1, 1), :] + R

    def coded(points, stride, first):
        row = lax.broadcasted_iota(jnp.int32, (points, K), 0) * stride + first
        col = lax.broadcasted_iota(jnp.int32, (points, K), 1)
        hit = jnp.where(row == col, jnp.broadcast_to(code, (points, K)).astype(f32), 0.0)
        own = jnp.sum(hit, axis=1, keepdims=True).astype(jnp.int32)
        return jnp.broadcast_to(own, (points, N))

    codes[...] = coded(K, 1, 0)
    half = lax.broadcasted_iota(jnp.int32, (K // 2, N), 1) < C
    code_pairs[...] = jnp.where(half, coded(K // 2, 2, 0), coded(K // 2, 2, 1))

    def place(p, carry):
        plain = jnp.zeros((C, N), f32)
        turned = jnp.zeros((C, N), f32)
        for k in range(K):
            mine = codes[pl.ds(k, 1), :] == p
            plain = plain + jnp.where(mine, wide[k], 0.0)
            turned = turned + jnp.where(mine, wide_t[k], 0.0)
        w5[p] = plain.astype(bf16)
        w5t[p] = turned.astype(bf16)
        return carry

    lax.fori_loop(0, W * W, place, 0)
    nothing = jnp.zeros((C, N), bf16)

    def band(o, carry):
        for s in range(GROUP):
            for j in range(BAND // 2):
                ahead, back = [], []
                for r in (2 * j, 2 * j + 1):
                    a = r - s
                    inside = 0 <= a < W
                    ahead.append(w5t[a * W + o] if inside else nothing)
                    back.append(w5[(W - 1 - a) * W + (W - 1 - o)] if inside else nothing)
                cols = pl.ds(pl.multiple_of(o * BAND * C + j * N, N), N)
                fwd[pl.ds(s * C, C), cols] = jnp.where(low, ahead[0], ahead[1])
                bwd[pl.ds(s * C, C), cols] = jnp.where(low, back[0], back[1])
        return carry

    lax.fori_loop(0, W, band, 0)

    loads[2].wait()
    lane8 = lax.broadcasted_iota(jnp.int32, (L, N), 1)
    found = jnp.zeros((L, N), jnp.int32)
    for i in range(B):
        turned = pltpu.roll(abuf[i], lax.rem(N + i * B - gy * B, N), 1)
        found = jnp.where((lane8 >= i * B) & (lane8 < i * B + B), turned, found)
    rows = (found >> 7) - gx * B + B
    cols = (found & 127) - gy * B + B
    spot = ((rows >> 3) * 3 + (cols >> 3)) * C + (rows & 7) * B + (cols & 7)
    idx[...] = jnp.where(lane8 < C, spot, -1)

    def build_onehot(l, carry):
        target = lax.broadcasted_iota(jnp.int32, (TARGETS, N), 0)
        onehot[l] = jnp.where(target == idx[pl.ds(l, 1), :], 1.0, 0.0).astype(bf16)
        return carry

    lax.fori_loop(0, L, build_onehot, 0)

    t1_wait()
    top2[gx] = top1[:, 0, :]
    t2_start, t2_wait = line("gx", lambda p: top2.at[gx], lambda p: top2.at[p], t2_s, t2_r)
    t2_start()

    for copy in xhalo:
        copy.wait()
    finish_halo(xs, xright, xleft)

    for copy in coarse_copies:
        copy.wait()
    pieces = [
        jnp.where(low, coarse_nb[2 * j], coarse_nb[2 * j + 1] if j < 4 else nothing)
        for j in range(5)
    ]
    around_cells = jnp.concatenate(pieces, axis=1)

    def pick(l, total):
        chosen = dot(around_cells, onehot[l]).astype(bf16)
        picked[l] = chosen
        turned = lw[l].astype(f32).T.astype(bf16)
        return total + dot(turned, chosen)

    level_one = lax.fori_loop(0, L, pick, jnp.zeros((C, N), f32))
    t2_wait()
    me = gx * ny + gy
    top_all = top2[...].reshape(N, N)
    tw_f32 = tw[...].astype(f32)
    mixed = dot(tw_f32.T, top_all[:, :C], NT, HIGHEST)
    level_two = jnp.sum(mixed * tk[pl.ds(me, 1), :], axis=1, keepdims=True)
    spread_one = split_dot(level_one[:, :C], spread[pl.ds(0, C), :]) + level_two
    for i in range(B):
        base[i] = spread_one[:, i * N : (i + 1) * N]

    def banded(matrix, field, pair):
        parts = []
        for o in range(W):
            first = field[o, pl.ds(pair * 8, BAND)].reshape(BAND * C, N)
            second = field[o, pl.ds(pair * 8 + GROUP, BAND)].reshape(BAND * C, N)
            parts.append(jnp.concatenate([first, second], axis=1))
        return dot(matrix[...], jnp.concatenate(parts, axis=0))

    loads[1].wait()

    def forward(i, carry):
        rows16 = pl.ds(pl.multiple_of(i * CELL, CELL), CELL)
        upstream = jnp.swapaxes(cbuf[:, rows16, :], 0, 1)
        shared = base[i]
        actives, slopes = [], []
        total = jnp.zeros((C, N), f32)
        for half in range(2):
            near = banded(fwd, xs, i * 2 + half)
            for g in range(2):
                for s in range(GROUP):
                    x = half * 8 + g * GROUP + s
                    v = near[s * C : (s + 1) * C, g * N : (g + 1) * N] + shared
                    square = v * v
                    tangent = jnp.tanh(v * (root_scale + root_scale * cubic_term * square))
                    gate = 0.5 + 0.5 * tangent
                    actives.append(v * gate)
                    slope = gate + v * (gate - gate * gate) * (
                        2.0 * root_scale + 6.0 * root_scale * cubic_term * square
                    )
                    grad = (upstream[x].astype(f32) * slope).astype(bf16)
                    hs[R, R + i * CELL + x] = grad
                    slopes.append(grad)
                    total = total + grad.astype(f32)
        pooled[:, pl.ds(pl.multiple_of(i * N, N), N)] = total
        pack_edges(slopes, i, hpack)
        active = jnp.swapaxes(jnp.stack(actives), 0, 1)
        obuf[:, rows16, :] = (fbuf[:, rows16, :].astype(f32) + active).astype(bf16)
        pltpu.make_async_copy(
            obuf.at[:, rows16, :], out.at[:, rows16, :], store_sem.at[0, i]
        ).start()
        return carry

    lax.fori_loop(0, B, forward, 0)

    hhalo = halo_copies(hs, hpack, hright, hleft, hhalo_s, hhalo_r)
    for copy in hhalo:
        copy.start()

    one = split_dot(pooled[...], spread[...], NT)
    one_ref[...] = one
    two1[gy] = as_row(one)
    u1_start, u1_wait = line("gy", lambda p: two1.at[gy], lambda p: two1.at[p], u1_s, u1_r)
    u1_start()

    def push(l, total):
        grad = one_ref[...]
        pushed = dot_split(lw[l], grad)
        rs_src[l, pl.ds(C, C), :] = jnp.concatenate(
            [dot_split(picked[l], grad[:C, :], NT), jnp.zeros((C, N - C), f32)], axis=1
        )
        return total + split_dot(pushed, onehot[l], NT, 2)

    pushes = lax.fori_loop(0, L, push, jnp.zeros((C, TARGETS), f32))
    for j in range(5):
        ctr[j] = pushes[:, j * N : (j + 1) * N]
    push_copies = []
    for n, (dx, dy) in enumerate(around()):
        slot = (1 - dx) * 3 + (1 - dy)
        copy = pltpu.make_async_remote_copy(
            src_ref=ctr.at[(8 - slot) // 2], dst_ref=rctr.at[slot], send_sem=ct_s.at[n],
            recv_sem=ct_r.at[n], device_id=at(dx, dy), device_id_type=MESH,
        )
        copy.start()
        push_copies.append(copy)

    def weigh(step, carry):
        o = step // 2
        half = lax.rem(step, 2)
        left = jnp.concatenate(
            [
                xs[o, pl.ds(i * GROUP + half * GROUP, GROUP)].reshape(GROUP * C, N)
                for i in range(N // GROUP)
            ],
            axis=1,
        )
        right = jnp.concatenate(
            [
                hs[R, pl.ds(R + i * GROUP, GROUP)].reshape(GROUP * C, N)
                for i in range(N // GROUP)
            ],
            axis=1,
        )
        rows = pl.ds(pl.multiple_of(half * GROUP * C, GROUP * C), GROUP * C)
        grads[o, rows, :] = dot(left, right, NT)
        return carry

    lax.fori_loop(0, 4, weigh, 0)
    u1_wait()
    two2[gx] = two1[:, 0, :]
    u2_start, u2_wait = line("gx", lambda p: two2.at[gx], lambda p: two2.at[p], u2_s, u2_r)
    u2_start()
    lax.fori_loop(4, 2 * W, weigh, 0)

    def stencil_grad(p, carry):
        a = p // W
        b = lax.rem(p, W)
        part = [
            grads[b, pl.ds(pl.multiple_of((a + s) * C, C), C), pl.ds((s // 2) * N, N)]
            for s in range(GROUP)
        ]
        both = jnp.where(low, part[0] + part[2], part[1] + part[3])
        both = both + pltpu.roll(both, C, 1)
        for j in range(K // 2):
            mine = code_pairs[pl.ds(j, 1), :] == p
            rs_src[j, pl.ds(0, C), :] = jnp.where(mine, both, rs_src[j, pl.ds(0, C), :])
        return carry

    lax.fori_loop(0, W * W, stencil_grad, 0)
    rs1[gx] = rs_src[gx]
    r1_start, r1_wait = line("gx", lambda p: rs_src.at[p], lambda p: rs1.at[p], r1_s, r1_r)
    r1_start()

    for copy in hhalo:
        copy.wait()
    finish_halo(hs, hright, hleft)

    for copy in push_copies:
        copy.wait()
    evens = ctr[2]
    odds = jnp.zeros((C, N), f32)
    for slot in range(9):
        if slot == 4:
            continue
        if slot % 2 == 0:
            evens = evens + rctr[slot]
        else:
            odds = odds + rctr[slot]
    collected = evens + pltpu.roll(odds, C, 1)
    u2_wait()
    two_all = two2[...].reshape(N, N)[:, :C]
    kernel_grad = dot(tk[...], two_all, TN, HIGHEST)
    top_all = top2[...].reshape(N, N)
    top_out[...] = dot(top_all[:, :C], kernel_grad, TN, HIGHEST)
    mine = lax.broadcasted_iota(jnp.int32, (N, C), 0) == me
    kernel_row = jnp.sum(jnp.where(mine, kernel_grad, 0.0), axis=0, keepdims=True)
    top_coef_grad = jnp.sum(tw[...].astype(f32) * kernel_row, axis=1, keepdims=True)
    coarse_grad = (collected + top_coef_grad / B) / CELL
    spread_grad = split_dot(coarse_grad[:, :C], spread[pl.ds(0, C), :])
    for i in range(B):
        base[i] = spread_grad[:, i * N : (i + 1) * N]

    def backward(i, carry):
        rows16 = pl.ds(pl.multiple_of(i * CELL, CELL), CELL)
        shared = base[i]
        sums = []
        for half in range(2):
            near = banded(bwd, hs, i * 2 + half)
            for g in range(2):
                for s in range(GROUP):
                    sums.append(near[s * C : (s + 1) * C, g * N : (g + 1) * N] + shared)
        total = jnp.swapaxes(jnp.stack(sums), 0, 1)
        ibuf[:, rows16, :] = (cbuf[:, rows16, :].astype(f32) + total).astype(bf16)
        pltpu.make_async_copy(
            ibuf.at[:, rows16, :], ingrad.at[:, rows16, :], store_sem.at[1, i]
        ).start()
        return carry

    lax.fori_loop(0, 2, backward, 0)
    r1_wait()
    total = rs1[0]
    for j in range(1, nx):
        total = total + rs1[j]
    rs2_src[...] = total.reshape(ny, N // ny, N)
    rs2[gy] = rs2_src[gy]
    r2_start, r2_wait = line("gy", lambda p: rs2_src.at[p], lambda p: rs2.at[p], r2_s, r2_r)
    r2_start()
    lax.fori_loop(2, 4, backward, 0)
    r2_wait()
    total = rs2[0]
    for j in range(1, ny):
        total = total + rs2[j]
    ag1[gy] = total
    a1_start, a1_wait = line("gy", lambda p: ag1.at[gy], lambda p: ag1.at[p], a1_s, a1_r)
    a1_start()
    lax.fori_loop(4, 6, backward, 0)
    a1_wait()
    ag2[gx] = ag1[...].reshape(N, N)
    a2_start, a2_wait = line("gx", lambda p: ag2.at[gx], lambda p: ag2.at[p], a2_s, a2_r)
    a2_start()
    lax.fori_loop(6, B, backward, 0)
    a2_wait()
    for j in range(K // 2):
        near_out[2 * j] = ag2[j, pl.ds(0, C), pl.ds(0, C)]
        near_out[2 * j + 1] = ag2[j, pl.ds(0, C), pl.ds(C, C)]
        link_out[j] = ag2[j, pl.ds(C, C), pl.ds(0, C)]

    def drain(i, carry):
        rows16 = pl.ds(pl.multiple_of(i * CELL, CELL), CELL)
        pltpu.make_async_copy(
            obuf.at[:, rows16, :], out.at[:, rows16, :], store_sem.at[0, i]
        ).wait()
        pltpu.make_async_copy(
            ibuf.at[:, rows16, :], ingrad.at[:, rows16, :], store_sem.at[1, i]
        ).wait()
        return carry

    lax.fori_loop(0, B, drain, 0)


def solution(mesh):
    nx, ny = mesh.shape["gx"], mesh.shape["gy"]
    vmem = pl.BlockSpec(memory_space=pltpu.VMEM)
    anywhere = pl.BlockSpec(memory_space=pl.ANY)
    dma = pltpu.SemaphoreType.DMA

    def per_device(feat, cot, offsets, adjacency, near_w, link_w, top_w, top_k):
        scratch = [
            pltpu.VMEM((C, N, N), bf16),
            pltpu.VMEM((C, N, N), bf16),
            pltpu.VMEM((B, L, N), jnp.int32),
            pltpu.VMEM((W, HALO, C, N), bf16),
            pltpu.VMEM((W, HALO, C, N), bf16),
            pltpu.VMEM((2, 2, C, N), bf16),
            pltpu.VMEM((2, 2, C, N), bf16),
            pltpu.VMEM((4, C, N), bf16),
            pltpu.VMEM((4, C, N), bf16),
            pltpu.VMEM((4, C, N), bf16),
            pltpu.VMEM((4, C, N), bf16),
            pltpu.VMEM((K, C, N), f32),
            pltpu.VMEM((K, C, N), f32),
            pltpu.VMEM((W * W, C, N), bf16),
            pltpu.VMEM((W * W, C, N), bf16),
            pltpu.VMEM((GROUP * C, W * BAND * C), bf16),
            pltpu.VMEM((GROUP * C, W * BAND * C), bf16),
            pltpu.VMEM((N, B * N), bf16),
            pltpu.VMEM((C, B * N), f32),
            pltpu.VMEM((L, TARGETS, N), bf16),
            pltpu.VMEM((L, N), jnp.int32),
            pltpu.VMEM((9, C, N), bf16),
            pltpu.VMEM((L, C, N), bf16),
            pltpu.VMEM((B, C, N), f32),
            pltpu.VMEM((ny, 8, N), f32),
            pltpu.VMEM((nx, ny, N), f32),
            pltpu.VMEM((ny, 8, N), f32),
            pltpu.VMEM((nx, ny, N), f32),
            pltpu.VMEM((5, C, N), f32),
            pltpu.VMEM((9, C, N), f32),
            pltpu.VMEM((W, BAND * C, GROUP * C), f32),
            pltpu.VMEM((nx, N, N), f32),
            pltpu.VMEM((nx, N, N), f32),
            pltpu.VMEM((ny, N // ny, N), f32),
            pltpu.VMEM((ny, N // ny, N), f32),
            pltpu.VMEM((ny, N // ny, N), f32),
            pltpu.VMEM((nx, N, N), f32),
            pltpu.VMEM((C, N, N), bf16),
            pltpu.VMEM((C, N, N), bf16),
            pltpu.VMEM((C, N), f32),
            pltpu.VMEM((K, N), jnp.int32),
            pltpu.VMEM((K // 2, N), jnp.int32),
            dma((3,)),
            dma((2, B)),
            dma((8,)), dma((8,)), dma((8,)), dma((8,)),
            dma((8,)), dma((8,)), dma((8,)), dma((8,)),
            dma((ny,)), dma((ny,)), dma((nx,)), dma((nx,)),
            dma((ny,)), dma((ny,)), dma((nx,)), dma((nx,)),
            dma((nx,)), dma((nx,)), dma((ny,)), dma((ny,)),
            dma((ny,)), dma((ny,)), dma((nx,)), dma((nx,)),
        ]
        field = jax.ShapeDtypeStruct((C, N, N), bf16)
        return pl.pallas_call(
            functools.partial(kernel, nx, ny),
            out_shape=(
                field,
                field,
                jax.ShapeDtypeStruct((K, C, C), f32),
                jax.ShapeDtypeStruct((L, C, C), f32),
                jax.ShapeDtypeStruct((C, C), f32),
            ),
            in_specs=[
                anywhere, anywhere, anywhere,
                vmem, vmem, vmem, vmem, vmem,
            ],
            out_specs=(anywhere, anywhere, vmem, vmem, vmem),
            scratch_shapes=scratch,
            compiler_params=pltpu.CompilerParams(
                collective_id=0, has_side_effects=True, vmem_limit_bytes=60 * 2**20
            ),
        )(
            feat, cot, jnp.transpose(adjacency, (0, 2, 1)), offsets.T, near_w, link_w,
            top_w, top_k,
        )

    return jax.shard_map(
        per_device,
        mesh=mesh,
        in_specs=(P(None, "gx", "gy"), P(None, "gx", "gy"), P(), P(), P(), P(), P(), P()),
        out_specs=(P(None, "gx", "gy"), P(None, "gx", "gy"), P(), P(), P()),
        check_vma=False,
    )
```

time: 737 us -> 90.1 us (0.12); the launches traced: 727 us -> 89.9 us
  matrix products: 275 us -> 0 us
  local copies, waits for them, and re-layouts: 140 us -> 6.79 us
  loops' own time: 105 us -> 0 us
  other arithmetic: 93.8 us -> 0 us
  Pallas kernels: 0 us -> 82.5 us
  blocking collectives: 68 us -> 0 us
  starting transfers between devices: 31.3 us -> 0 us
  between operations: 14.6 us -> 0.66 us
    dot_general x56 -> x0, matrix products: 275 us -> none  [the longest x16 104 us: near_step(): jnp.einsum('cxy,cd->dxy', shifted, near_weight[offset_id], preferred_elem...]
    another operation x3 -> x0, loops' own time: 105 us -> none  [the longest x1 42 us: per_device(): lax.fori_loop(0, OFFSETS, weight_step, jnp.zeros((OFFSETS, channels, chan...]
    pallas_call x0 -> x1, Pallas kernels: none -> 82.5 us  [per_device(): pl.pallas_call(functools.partial(kernel, nx, ny), out_shape=(field, field...]
    unnamed x1 -> x0, blocking collectives: 68 us -> none
    unnamed x32 -> x13, local copies, waits for them, and re-layouts: 48.3 us -> 6.79 us
    ppermute x12 -> x0, starting transfers between devices: 31.2 us -> none  [the longest x6 21.4 us: with_halo(): lax.ppermute(lax.slice_in_dim(block, block.shape[dim] - width, None, axis...]
    dynamic_slice x50 -> x0, local copies, waits for them, and re-layouts: 29.5 us -> none  [the longest x16 10.6 us: back_step(): offsets[offset_id, 1]]
    scatter-add x1 -> x0, other arithmetic: 29.1 us -> none  [per_device(): collected = jnp.zeros((channels, own_cells + 1), jnp.float32).at[:, targe...]
  transfers between devices with their start and end apart: 14 -> 0, of which waited for: 0 -> 0; matrix products, arithmetic and copies ran while one was open for 60% -> 0% of each run, Pallas kernels for 0% -> 0%
where the time goes in v1:
time: 90.1 us; the launch traced here: 89.9 us
  Pallas kernels  82.5 us (92%)
  local copies, waits for them, and re-layouts  6.79 us (8%)
    pallas_call x1, Pallas kernels, per_device(): pl.pallas_call(functools.partial(kernel, nx, ny), out_shape=(field, field...  82.5 us
    unnamed x13, local copies, waits for them, and re-layouts  6.79 us

profile of v1, /device:TPU:1, one launch (start us, length us, event | category | flops | bytes accessed | tf_op | source)
XLA Modules:
  0.0 89.9 jit_solution(10550872935539902082)
XLA Ops:
  0.6 82.5 %shard_map.119 = (bf16[64,128,128]{2,1,0:T(8,128)(2,1)}, bf16[64,128,128]{2,1,0:T(8,128)(2,1)}, f32[16,64,64]{2,1,0:T(8,128)}, f32[8,64,64]{2,1,0:T(8,128)}, f32[64,64]{1,0:T(8,128)}) custom-call(bf16[64,128,128]{2,1,0:T(8,128)(2,1)} %feat.1, bf16[64,128,128]{2,1,0:T(8,128)(2,1)} %cot.1, s32[64,8,128]{2,1,0:T(8,128)} %bitcast.2, s32[2,16]{1,0:T(2,128)} %bitcast.3, ...), custom_call_target="tpu_custom_call" | custom-call | tf_op jit(solution)/shard_map/pallas_call | solution.py:614
  83.1 0.0 copy-start
  83.1 3.3 %copy.18 = bf16[64,128,128]{2,1,0:T(8,128)(2,1)} copy(bf16[64,128,128]{2,1,0:T(8,128)(2,1)} %get-tuple-element.10) | data formatting | bytes 4194304
  86.4 0.0 copy-done
  86.4 0.0 copy-start.1
  86.4 0.0 copy-start.2
  86.4 0.0 copy-start.3
  86.4 1.3 %copy.19 = bf16[64,128,128]{2,1,0:T(8,128)(2,1)} copy(bf16[64,128,128]{2,1,0:T(8,128)(2,1)S(1)} %copy-done) | data formatting | bytes 4194304
  87.8 0.0 copy-done.1
  87.8 0.8 copy.20
  88.6 0.0 copy-done.2
  88.6 0.7 copy.21
  89.3 0.0 copy-done.3
  89.3 0.6 copy.22
Async XLA Ops:
  83.1 3.3 %copy-start = (bf16[64,128,128]{2,1,0:T(8,128)(2,1)S(1)}, bf16[64,128,128]{2,1,0:T(8,128)(2,1)}, u32[]{:S(2)}) copy-start(bf16[64,128,128]{2,1,0:T(8,128)(2,1)} %get-tuple-element.11) | copy-start | bytes 6291460
  86.4 1.4 %copy-start.1 = (f32[16,64,64]{2,1,0:T(8,128)S(1)}, f32[16,64,64]{2,1,0:T(8,128)}, u32[]{:S(2)}) copy-start(f32[16,64,64]{2,1,0:T(8,128)} %get-tuple-element.12) | copy-start | bytes 786436
  86.4 2.2 %copy-start.2 = (f32[8,64,64]{2,1,0:T(8,128)S(1)}, f32[8,64,64]{2,1,0:T(8,128)}, u32[]{:S(2)}) copy-start(f32[8,64,64]{2,1,0:T(8,128)} %get-tuple-element.13) | copy-start | bytes 393220
  86.4 2.9 %copy-start.3 = (f32[64,64]{1,0:T(8,128)S(1)}, f32[64,64]{1,0:T(8,128)}, u32[]{:S(2)}) copy-start(f32[64,64]{1,0:T(8,128)} %get-tuple-element.14) | copy-start | bytes 49156

commit v2 on v1

--- a/solution.py
+++ b/solution.py
@@ -18,6 +18,7 @@
 HALO = N + 2 * R
 GROUP = 4
 BAND = GROUP + 2 * R
+SLABS = 66
 TARGETS = 640
 
 root_scale = 0.7978845608028654
@@ -58,15 +59,15 @@
 
 def kernel(
     nx, ny,
-    feat, cot, adj, offs, nw, lw, tw, tk,
-    out, ingrad, near_out, link_out, top_out,
+    feat, cot, adj, offs, spots, nw, lw, tw, tk,
+    obuf, ibuf, near_out, link_out, top_out,
     fbuf, cbuf, abuf, xs, hs, xpack, hpack, xright, xleft, hright, hleft,
     wide, wide_t, w5, w5t, fwd, bwd, spread, pooled, onehot, idx,
     coarse_nb, picked, base, top1, top2, two1, two2, ctr, rctr, grads,
-    rs_src, rs1, rs2_src, rs2, ag1, ag2, obuf, ibuf, one_ref, codes, code_pairs,
-    load_sem, store_sem, halo_s, halo_r, hhalo_s, hhalo_r, co_s, co_r, ct_s, ct_r,
+    rs_src, rs1, rs2, ag, one_ref, codes, mover, edges, near_buf, stencil,
+    load_sem, halo_s, halo_r, hhalo_s, hhalo_r, co_s, co_r, ct_s, ct_r,
     t1_s, t1_r, t2_s, t2_r, u1_s, u1_r, u2_s, u2_r,
-    r1_s, r1_r, r2_s, r2_r, a1_s, a1_r, a2_s, a2_r,
+    r1_s, r1_r, r2_s, r2_r, a1_s, a1_r,
 ):
     gx = lax.axis_index("gx")
     gy = lax.axis_index("gy")
@@ -102,8 +103,12 @@
         return carry
 
     lax.fori_loop(0, B, build_spread, 0)
+    source = lax.broadcasted_iota(jnp.int32, (2 * N, N), 0)
+    for n, o in enumerate((0, 1, 3, 4)):
+        y = lax.broadcasted_iota(jnp.int32, (2 * N, N), 1) + (o - R)
+        y = jnp.where(y < 0, y + N + R, jnp.where(y >= N, y + C, y))
+        mover[:, n * N : (n + 1) * N] = jnp.where(source == y, 1.0, 0.0).astype(bf16)
     xpack[...] = jnp.zeros_like(xpack)
-    rs_src[...] = jnp.zeros_like(rs_src)
     hpack[...] = jnp.zeros_like(hpack)
 
     def pack_edges(block, i, pack):
@@ -114,10 +119,10 @@
             first = jnp.where((lane >= 2 * x) & (lane < 2 * x + 2), turned, first)
             spot = (2 * x - 2) % N
             last = jnp.where((lane >= spot) & (lane < spot + 2), turned, last)
-        shift = 2 * CELL * lax.rem(i, 4) + 2
+        shift = 2 * CELL * lax.rem(i, 4)
         half = i // 4
         pack[0, half] = pack[0, half] + pltpu.roll(first, shift, 1)
-        pack[1, half] = pack[1, half] + pltpu.roll(last, shift, 1)
+        pack[1, half] = pack[1, half] + pltpu.roll(last, shift + 2, 1)
 
     loads[0].wait()
 
@@ -163,22 +168,30 @@
             for part, there in ((0, inside & up), (1, inside), (2, inside), (3, inside & down)):
                 side[part] = jnp.where(there, side[part], jnp.zeros((C, N), bf16))
 
+        for part in range(4):
+            for half in range(2):
+                one, two = (left[part], pltpu.roll(right[part], C, 1))
+                if half:
+                    one, two = (pltpu.roll(left[part], C, 1), right[part])
+                edges[2 * part + half] = jnp.where(low, one, two)
+
         def shift(step, carry):
-            for n in range(4):
-                t = step * 4 + n
+            rows = []
+            for n in range(SLABS):
+                t = step * SLABS + n
                 place = t + (C - R)
-                part = place // C
-                s = 2 * lax.rem(place, C) + 2
-                mixed = jnp.where(((lane - (s - 2)) & (N - 1)) < 2, left[part], right[part])
-                edge = pltpu.roll(mixed, lax.rem(2 * N - s, N), 1)
-                slab = field[R, t]
-                field[0, t] = pltpu.roll(jnp.where(lane >= N - 2, edge, slab), 2, 1)
-                field[1, t] = pltpu.roll(jnp.where(lane >= N - 1, edge, slab), 1, 1)
-                field[3, t] = pltpu.roll(jnp.where(lane < 1, edge, slab), N - 1, 1)
-                field[4, t] = pltpu.roll(jnp.where(lane < 2, edge, slab), N - 2, 1)
+                turn = lax.rem(N - 2 * lax.rem(place, 32), N)
+                rows.append(
+                    jnp.concatenate([field[R, t], pltpu.roll(edges[place // 32], turn, 1)], axis=1)
+                )
+            moved = dot(jnp.concatenate(rows, axis=0), mover[...]).astype(bf16)
+            for n, o in enumerate((0, 1, 3, 4)):
+                field[o, pl.ds(step * SLABS, SLABS)] = moved[:, n * N : (n + 1) * N].reshape(
+                    SLABS, C, N
+                )
             return carry
 
-        lax.fori_loop(0, HALO // 4, shift, 0)
+        lax.fori_loop(0, HALO // SLABS, shift, 0)
 
     def around():
         return [(dx, dy) for dx in (-1, 0, 1) for dy in (-1, 0, 1) if (dx, dy) != (0, 0)]
@@ -212,13 +225,53 @@
 
         return start, wait
 
+    coarse = (split_dot(pooled[...], spread[...], NT) / CELL).astype(bf16)
+    coarse_nb[4] = coarse
+    ones = jnp.where(lax.broadcasted_iota(jnp.int32, (8, N), 1) < C, 1.0, 0.0)
+
+    def as_row(values):
+        sums = dot(ones, values, NT, HIGHEST)
+        return jnp.concatenate([sums, jnp.zeros((8, N - C), f32)], axis=1)
+
+    top1[gy] = as_row(coarse.astype(f32)) / B
+
+    def widen(k, carry):
+        block = nw[k].astype(f32)
+        wide[k] = jnp.concatenate([block, block], axis=1)
+        turned = block.T
+        wide_t[k] = jnp.concatenate([turned, turned], axis=1)
+        return carry
+
+    lax.fori_loop(0, K, widen, 0, unroll=4)
+
+    code = (offs[pl.ds(0, 1), :] + R) * W + offs[pl.ds(1, 1), :] + R
+
+    def coded(points, stride, first):
+        row = lax.broadcasted_iota(jnp.int32, (points, K), 0) * stride + first
+        col = lax.broadcasted_iota(jnp.int32, (points, K), 1)
+        hit = jnp.where(row == col, jnp.broadcast_to(code, (points, K)).astype(f32), 0.0)
+        own = jnp.sum(hit, axis=1, keepdims=True).astype(jnp.int32)
+        return jnp.broadcast_to(own, (points, N))
+
+    codes[...] = coded(K, 1, 0)
+
+    def place(p, carry):
+        plain = jnp.zeros((C, N), f32)
+        turned = jnp.zeros((C, N), f32)
+        for k in range(K):
+            mine = codes[pl.ds(k, 1), :] == p
+            plain = plain + jnp.where(mine, wide[k], 0.0)
+            turned = turned + jnp.where(mine, wide_t[k], 0.0)
+        w5[p] = plain.astype(bf16)
+        w5t[p] = turned.astype(bf16)
+        return carry
+
+    lax.fori_loop(0, W * W, place, 0, unroll=5)
     pl.semaphore_wait(barrier, nx - 1 + ny - 1 + 4)
     xhalo = halo_copies(xs, xpack, xright, xleft, halo_s, halo_r)
     for copy in xhalo:
         copy.start()
 
-    coarse = (split_dot(pooled[...], spread[...], NT) / CELL).astype(bf16)
-    coarse_nb[4] = coarse
     coarse_copies = []
     for n, (dx, dy) in enumerate(around()):
         slot = (1 - dx) * 3 + (1 - dy)
@@ -228,50 +281,9 @@
         )
         copy.start()
         coarse_copies.append(copy)
-    ones = jnp.where(lax.broadcasted_iota(jnp.int32, (8, N), 1) < C, 1.0, 0.0)
-
-    def as_row(values):
-        sums = dot(ones, values, NT, HIGHEST)
-        return jnp.concatenate([sums, jnp.zeros((8, N - C), f32)], axis=1)
-
-    top1[gy] = as_row(coarse.astype(f32)) / B
     t1_start, t1_wait = line("gy", lambda p: top1.at[gy], lambda p: top1.at[p], t1_s, t1_r)
     t1_start()
 
-    def widen(k, carry):
-        block = nw[k].astype(f32)
-        wide[k] = jnp.concatenate([block, block], axis=1)
-        turned = block.T
-        wide_t[k] = jnp.concatenate([turned, turned], axis=1)
-        return carry
-
-    lax.fori_loop(0, K, widen, 0)
-
-    code = (offs[pl.ds(0, 1), :] + R) * W + offs[pl.ds(1, 1), :] + R
-
-    def coded(points, stride, first):
-        row = lax.broadcasted_iota(jnp.int32, (points, K), 0) * stride + first
-        col = lax.broadcasted_iota(jnp.int32, (points, K), 1)
-        hit = jnp.where(row == col, jnp.broadcast_to(code, (points, K)).astype(f32), 0.0)
-        own = jnp.sum(hit, axis=1, keepdims=True).astype(jnp.int32)
-        return jnp.broadcast_to(own, (points, N))
-
-    codes[...] = coded(K, 1, 0)
-    half = lax.broadcasted_iota(jnp.int32, (K // 2, N), 1) < C
-    code_pairs[...] = jnp.where(half, coded(K // 2, 2, 0), coded(K // 2, 2, 1))
-
-    def place(p, carry):
-        plain = jnp.zeros((C, N), f32)
-        turned = jnp.zeros((C, N), f32)
-        for k in range(K):
-            mine = codes[pl.ds(k, 1), :] == p
-            plain = plain + jnp.where(mine, wide[k], 0.0)
-            turned = turned + jnp.where(mine, wide_t[k], 0.0)
-        w5[p] = plain.astype(bf16)
-        w5t[p] = turned.astype(bf16)
-        return carry
-
-    lax.fori_loop(0, W * W, place, 0)
     nothing = jnp.zeros((C, N), bf16)
 
     def band(o, carry):
@@ -288,7 +300,7 @@
                 bwd[pl.ds(s * C, C), cols] = jnp.where(low, back[0], back[1])
         return carry
 
-    lax.fori_loop(0, W, band, 0)
+    lax.fori_loop(0, W, band, 0, unroll=True)
 
     loads[2].wait()
     lane8 = lax.broadcasted_iota(jnp.int32, (L, N), 1)
@@ -331,7 +343,20 @@
         turned = lw[l].astype(f32).T.astype(bf16)
         return total + dot(turned, chosen)
 
-    level_one = lax.fori_loop(0, L, pick, jnp.zeros((C, N), f32))
+    level_one = lax.fori_loop(0, L, pick, jnp.zeros((C, N), f32), unroll=True)
+    def banded(matrix, field, pair):
+        parts = []
+        for o in range(W):
+            first = field[o, pl.ds(pair * 8, BAND)].reshape(BAND * C, N)
+            second = field[o, pl.ds(pair * 8 + GROUP, BAND)].reshape(BAND * C, N)
+            parts.append(jnp.concatenate([first, second], axis=1))
+        return dot(matrix[...], jnp.concatenate(parts, axis=0))
+
+    def near_field(pair, carry):
+        near_buf[pair] = banded(fwd, xs, pair)
+        return carry
+
+    lax.fori_loop(0, N // (2 * GROUP), near_field, 0, unroll=True)
     t2_wait()
     me = gx * ny + gy
     top_all = top2[...].reshape(N, N)
@@ -342,14 +367,6 @@
     for i in range(B):
         base[i] = spread_one[:, i * N : (i + 1) * N]
 
-    def banded(matrix, field, pair):
-        parts = []
-        for o in range(W):
-            first = field[o, pl.ds(pair * 8, BAND)].reshape(BAND * C, N)
-            second = field[o, pl.ds(pair * 8 + GROUP, BAND)].reshape(BAND * C, N)
-            parts.append(jnp.concatenate([first, second], axis=1))
-        return dot(matrix[...], jnp.concatenate(parts, axis=0))
-
     loads[1].wait()
 
     def forward(i, carry):
@@ -359,11 +376,11 @@
         actives, slopes = [], []
         total = jnp.zeros((C, N), f32)
         for half in range(2):
-            near = banded(fwd, xs, i * 2 + half)
             for g in range(2):
                 for s in range(GROUP):
                     x = half * 8 + g * GROUP + s
-                    v = near[s * C : (s + 1) * C, g * N : (g + 1) * N] + shared
+                    near = near_buf[i * 2 + half, pl.ds(s * C, C), pl.ds(g * N, N)]
+                    v = near + shared
                     square = v * v
                     tangent = jnp.tanh(v * (root_scale + root_scale * cubic_term * square))
                     gate = 0.5 + 0.5 * tangent
@@ -379,9 +396,6 @@
         pack_edges(slopes, i, hpack)
         active = jnp.swapaxes(jnp.stack(actives), 0, 1)
         obuf[:, rows16, :] = (fbuf[:, rows16, :].astype(f32) + active).astype(bf16)
-        pltpu.make_async_copy(
-            obuf.at[:, rows16, :], out.at[:, rows16, :], store_sem.at[0, i]
-        ).start()
         return carry
 
     lax.fori_loop(0, B, forward, 0)
@@ -396,15 +410,63 @@
     u1_start, u1_wait = line("gy", lambda p: two1.at[gy], lambda p: two1.at[p], u1_s, u1_r)
     u1_start()
 
+    left = jnp.concatenate(
+        [
+            jnp.concatenate(
+                [xs[o, pl.ds(i * GROUP, BAND)].reshape(BAND * C, N) for i in range(N // GROUP)],
+                axis=1,
+            )
+            for o in range(W)
+        ],
+        axis=0,
+    )
+    right = jnp.concatenate(
+        [hs[R, pl.ds(R + i * GROUP, GROUP)].reshape(GROUP * C, N) for i in range(N // GROUP)],
+        axis=1,
+    )
+    grads[...] = dot(left, right, NT).reshape(W, BAND * C, GROUP * C)
+    u1_wait()
+    two2[gx] = two1[:, 0, :]
+    u2_start, u2_wait = line("gx", lambda p: two2.at[gx], lambda p: two2.at[p], u2_s, u2_r)
+    u2_start()
+
+    def stencil_grad(p, carry):
+        a = p // W
+        b = lax.rem(p, W)
+        part = [
+            grads[b, pl.ds(pl.multiple_of((a + s) * C, C), C), pl.ds((s // 2) * N, N)]
+            for s in range(GROUP)
+        ]
+        both = jnp.where(low, part[0] + part[2], part[1] + part[3])
+        both = both + pltpu.roll(both, C, 1)
+        stencil[p] = jnp.where(low[:32], both[:32], both[32:])
+        return carry
+
+    lax.fori_loop(0, W * W, stencil_grad, 0, unroll=True)
+
+    for k in range(K):
+        rs_src[k, pl.ds(0, 32), :] = stencil[(spots[0, k] + R) * W + spots[1, k] + R].astype(bf16)
+
+    def link_grads(l, carry):
+        grad = dot_split(picked[l], one_ref[...], NT)
+        for half in range(2):
+            rows = [grad[(2 * half + n) * 16 : (2 * half + n + 1) * 16] for n in range(2)]
+            rs_src[2 * l + half, pl.ds(32, 16), :] = jnp.concatenate(
+                [rows[0][:, :C], rows[1][:, :C]], axis=1
+            ).astype(bf16)
+        return carry
+
+    lax.fori_loop(0, L, link_grads, 0, unroll=True)
+    rs1[gy] = rs_src[gy]
+    r1_start, r1_wait = line("gy", lambda p: rs_src.at[p], lambda p: rs1.at[p], r1_s, r1_r)
+    r1_start()
+
     def push(l, total):
         grad = one_ref[...]
         pushed = dot_split(lw[l], grad)
-        rs_src[l, pl.ds(C, C), :] = jnp.concatenate(
-            [dot_split(picked[l], grad[:C, :], NT), jnp.zeros((C, N - C), f32)], axis=1
-        )
         return total + split_dot(pushed, onehot[l], NT, 2)
 
-    pushes = lax.fori_loop(0, L, push, jnp.zeros((C, TARGETS), f32))
+    pushes = lax.fori_loop(0, L, push, jnp.zeros((C, TARGETS), f32), unroll=True)
     for j in range(5):
         ctr[j] = pushes[:, j * N : (j + 1) * N]
     push_copies = []
@@ -416,53 +478,6 @@
         )
         copy.start()
         push_copies.append(copy)
-
-    def weigh(step, carry):
-        o = step // 2
-        half = lax.rem(step, 2)
-        left = jnp.concatenate(
-            [
-                xs[o, pl.ds(i * GROUP + half * GROUP, GROUP)].reshape(GROUP * C, N)
-                for i in range(N // GROUP)
-            ],
-            axis=1,
-        )
-        right = jnp.concatenate(
-            [
-                hs[R, pl.ds(R + i * GROUP, GROUP)].reshape(GROUP * C, N)
-                for i in range(N // GROUP)
-            ],
-            axis=1,
-        )
-        rows = pl.ds(pl.multiple_of(half * GROUP * C, GROUP * C), GROUP * C)
-        grads[o, rows, :] = dot(left, right, NT)
-        return carry
-
-    lax.fori_loop(0, 4, weigh, 0)
-    u1_wait()
-    two2[gx] = two1[:, 0, :]
-    u2_start, u2_wait = line("gx", lambda p: two2.at[gx], lambda p: two2.at[p], u2_s, u2_r)
-    u2_start()
-    lax.fori_loop(4, 2 * W, weigh, 0)
-
-    def stencil_grad(p, carry):
-        a = p // W
-        b = lax.rem(p, W)
-        part = [
-            grads[b, pl.ds(pl.multiple_of((a + s) * C, C), C), pl.ds((s // 2) * N, N)]
-            for s in range(GROUP)
-        ]
-        both = jnp.where(low, part[0] + part[2], part[1] + part[3])
-        both = both + pltpu.roll(both, C, 1)
-        for j in range(K // 2):
-            mine = code_pairs[pl.ds(j, 1), :] == p
-            rs_src[j, pl.ds(0, C), :] = jnp.where(mine, both, rs_src[j, pl.ds(0, C), :])
-        return carry
-
-    lax.fori_loop(0, W * W, stencil_grad, 0)
-    rs1[gx] = rs_src[gx]
-    r1_start, r1_wait = line("gx", lambda p: rs_src.at[p], lambda p: rs1.at[p], r1_s, r1_r)
-    r1_start()
 
     for copy in hhalo:
         copy.wait()
@@ -504,51 +519,44 @@
                     sums.append(near[s * C : (s + 1) * C, g * N : (g + 1) * N] + shared)
         total = jnp.swapaxes(jnp.stack(sums), 0, 1)
         ibuf[:, rows16, :] = (cbuf[:, rows16, :].astype(f32) + total).astype(bf16)
-        pltpu.make_async_copy(
-            ibuf.at[:, rows16, :], ingrad.at[:, rows16, :], store_sem.at[1, i]
-        ).start()
-        return carry
-
-    lax.fori_loop(0, 2, backward, 0)
+        return carry
+
+    lax.fori_loop(0, 3, backward, 0, unroll=True)
     r1_wait()
-    total = rs1[0]
+    total = rs1[0].astype(f32)
+    for j in range(1, ny):
+        total = total + rs1[j].astype(f32)
+    rs2[gx] = total.astype(bf16)
+    r2_start, r2_wait = line("gx", lambda p: rs2.at[gx], lambda p: rs2.at[p], r2_s, r2_r)
+    r2_start()
+    lax.fori_loop(3, 6, backward, 0, unroll=True)
+    r2_wait()
+    total = rs2[0].astype(f32)
     for j in range(1, nx):
-        total = total + rs1[j]
-    rs2_src[...] = total.reshape(ny, N // ny, N)
-    rs2[gy] = rs2_src[gy]
-    r2_start, r2_wait = line("gy", lambda p: rs2_src.at[p], lambda p: rs2.at[p], r2_s, r2_r)
-    r2_start()
-    lax.fori_loop(2, 4, backward, 0)
-    r2_wait()
-    total = rs2[0]
-    for j in range(1, ny):
-        total = total + rs2[j]
-    ag1[gy] = total
-    a1_start, a1_wait = line("gy", lambda p: ag1.at[gy], lambda p: ag1.at[p], a1_s, a1_r)
+        total = total + rs2[j].astype(f32)
+    ag[gy] = total.astype(bf16)
+    a1_start, a1_wait = line("gy", lambda p: ag.at[gy], lambda p: ag.at[p], a1_s, a1_r)
     a1_start()
-    lax.fori_loop(4, 6, backward, 0)
+    lax.fori_loop(6, B, backward, 0, unroll=True)
     a1_wait()
-    ag2[gx] = ag1[...].reshape(N, N)
-    a2_start, a2_wait = line("gx", lambda p: ag2.at[gx], lambda p: ag2.at[p], a2_s, a2_r)
-    a2_start()
-    lax.fori_loop(6, B, backward, 0)
-    a2_wait()
-    for j in range(K // 2):
-        near_out[2 * j] = ag2[j, pl.ds(0, C), pl.ds(0, C)]
-        near_out[2 * j + 1] = ag2[j, pl.ds(0, C), pl.ds(C, C)]
-        link_out[j] = ag2[j, pl.ds(C, C), pl.ds(0, C)]
-
-    def drain(i, carry):
-        rows16 = pl.ds(pl.multiple_of(i * CELL, CELL), CELL)
-        pltpu.make_async_copy(
-            obuf.at[:, rows16, :], out.at[:, rows16, :], store_sem.at[0, i]
-        ).wait()
-        pltpu.make_async_copy(
-            ibuf.at[:, rows16, :], ingrad.at[:, rows16, :], store_sem.at[1, i]
-        ).wait()
-        return carry
-
-    lax.fori_loop(0, B, drain, 0)
+    for k in range(K):
+        whole = ag[k].astype(f32)
+        near_out[k, pl.ds(0, 32), :] = whole[:32, :C]
+        near_out[k, pl.ds(32, 32), :] = pltpu.roll(whole[:32], C, 1)[:, :C]
+        link_out[k // 2, pl.ds((k % 2) * 32, 16), :] = whole[32:, :C]
+        link_out[k // 2, pl.ds((k % 2) * 32 + 16, 16), :] = pltpu.roll(whole[32:], C, 1)[:, :C]
+
+
+def store(*refs):
+    count = len(refs) // 2
+    sems = refs[-1]
+    copies = [
+        pltpu.make_async_copy(refs[n], refs[count + n], sems.at[n]) for n in range(count)
+    ]
+    for copy in copies:
+        copy.start()
+    for copy in copies:
+        copy.wait()
 
 
 def solution(mesh):
@@ -590,49 +598,56 @@
             pltpu.VMEM((5, C, N), f32),
             pltpu.VMEM((9, C, N), f32),
             pltpu.VMEM((W, BAND * C, GROUP * C), f32),
-            pltpu.VMEM((nx, N, N), f32),
-            pltpu.VMEM((nx, N, N), f32),
-            pltpu.VMEM((ny, N // ny, N), f32),
-            pltpu.VMEM((ny, N // ny, N), f32),
-            pltpu.VMEM((ny, N // ny, N), f32),
-            pltpu.VMEM((nx, N, N), f32),
-            pltpu.VMEM((C, N, N), bf16),
-            pltpu.VMEM((C, N, N), bf16),
+            pltpu.VMEM((ny, 48, N), bf16),
+            pltpu.VMEM((ny, 48, N), bf16),
+            pltpu.VMEM((nx, 48, N), bf16),
+            pltpu.VMEM((ny, 48, N), bf16),
             pltpu.VMEM((C, N), f32),
             pltpu.VMEM((K, N), jnp.int32),
-            pltpu.VMEM((K // 2, N), jnp.int32),
+            pltpu.VMEM((2 * N, 4 * N), bf16),
+            pltpu.VMEM((8, C, N), bf16),
+            pltpu.VMEM((N // (2 * GROUP), GROUP * C, 2 * N), f32),
+            pltpu.VMEM((W * W, 32, N), f32),
             dma((3,)),
-            dma((2, B)),
             dma((8,)), dma((8,)), dma((8,)), dma((8,)),
             dma((8,)), dma((8,)), dma((8,)), dma((8,)),
             dma((ny,)), dma((ny,)), dma((nx,)), dma((nx,)),
             dma((ny,)), dma((ny,)), dma((nx,)), dma((nx,)),
-            dma((nx,)), dma((nx,)), dma((ny,)), dma((ny,)),
-            dma((ny,)), dma((ny,)), dma((nx,)), dma((nx,)),
+            dma((ny,)), dma((ny,)), dma((nx,)), dma((nx,)), dma((ny,)), dma((ny,)),
         ]
-        field = jax.ShapeDtypeStruct((C, N, N), bf16)
-        return pl.pallas_call(
+        results = (
+            ((C, N, N), bf16),
+            ((C, N, N), bf16),
+            ((K, C, C), f32),
+            ((L, C, C), f32),
+            ((C, C), f32),
+        )
+        held = pl.pallas_call(
             functools.partial(kernel, nx, ny),
-            out_shape=(
-                field,
-                field,
-                jax.ShapeDtypeStruct((K, C, C), f32),
-                jax.ShapeDtypeStruct((L, C, C), f32),
-                jax.ShapeDtypeStruct((C, C), f32),
-            ),
+            out_shape=[pltpu.VMEM(*result) for result in results],
             in_specs=[
                 anywhere, anywhere, anywhere,
-                vmem, vmem, vmem, vmem, vmem,
+                vmem,
+                pl.BlockSpec(memory_space=pltpu.SMEM),
+                vmem, vmem, vmem, vmem,
             ],
-            out_specs=(anywhere, anywhere, vmem, vmem, vmem),
+            out_specs=[vmem] * 5,
             scratch_shapes=scratch,
             compiler_params=pltpu.CompilerParams(
-                collective_id=0, has_side_effects=True, vmem_limit_bytes=60 * 2**20
+                collective_id=0, has_side_effects=True, vmem_limit_bytes=54 * 2**20
             ),
         )(
-            feat, cot, jnp.transpose(adjacency, (0, 2, 1)), offsets.T, near_w, link_w,
+            feat, cot, jnp.transpose(adjacency, (0, 2, 1)), offsets.T, offsets.T, near_w, link_w,
             top_w, top_k,
         )
+        return pl.pallas_call(
+            store,
+            out_shape=[jax.ShapeDtypeStruct(*result) for result in results],
+            in_specs=[vmem] * 5,
+            out_specs=[anywhere] * 5,
+            scratch_shapes=[dma((5,))],
+            compiler_params=pltpu.CompilerParams(vmem_limit_bytes=2**20),
+        )(*[pltpu.with_memory_space_constraint(value, pltpu.VMEM) for value in held])
 
     return jax.shard_map(
         per_device,

time: 90.1 us -> 70 us (0.78)
  Pallas kernels: 82.5 us -> 69 us
  local copies, waits for them, and re-layouts: 6.79 us -> 0 us
    pallas_call x1 -> x2, Pallas kernels: 82.5 us -> 69 us  [the longest x1 66.8 us: per_device(): pl.pallas_call(functools.partial(kernel, nx, ny), out_shape=[pltpu.VMEM(*...]
    unnamed x13 -> x0, local copies, waits for them, and re-layouts: 6.79 us -> none
where the time goes in v2:
time: 70 us; the launch traced here: 69.9 us
  Pallas kernels  69 us (99%)
  between operations  0.82 us (1%)
    pallas_call x1, Pallas kernels, per_device(): pl.pallas_call(functools.partial(kernel, nx, ny), out_shape=[pltpu.VMEM(*...  66.8 us
    pallas_call x1, Pallas kernels, per_device(): pl.pallas_call(store, out_shape=[jax.ShapeDtypeStruct(*result) for result...  2.29 us

profile of v2, /device:TPU:1, one launch (start us, length us, event | category | flops | bytes accessed | tf_op | source)
XLA Modules:
  0.0 69.9 jit_solution(3467964559563661211)
XLA Ops:
  0.6 66.8 %shard_map.119 = (bf16[64,128,128]{2,1,0:T(8,128)(2,1)S(1)}, bf16[64,128,128]{2,1,0:T(8,128)(2,1)S(1)}, f32[16,64,64]{2,1,0:T(8,128)S(1)}, f32[8,64,64]{2,1,0:T(8,128)S(1)}, f32[64,64]{1,0:T(8,128)S(1)}) custom-call(bf16[64,128,128]{2,1,0:T(8,128)(2,1)} %feat.1, bf16[64,128,128]{2,1,0:T(8,128)(2,1)} %cot.1, s32[64,8,128]{2,1,0:T(8,128)} %bitcast.2, ...), custom_call_target="tpu_custom_call" | custom-call | tf_op jit(solution)/shard_map/pallas_call | solution.py:625
  67.4 2.3 %shard_map.120 = (bf16[64,128,128]{2,1,0:T(8,128)(2,1)}, bf16[64,128,128]{2,1,0:T(8,128)(2,1)}, f32[16,64,64]{2,1,0:T(8,128)}, f32[8,64,64]{2,1,0:T(8,128)}, f32[64,64]{1,0:T(8,128)}) custom-call(bf16[64,128,128]{2,1,0:T(8,128)(2,1)S(1)} %get-tuple-element.10.refs_0_, bf16[64,128,128]{2,1,0:T(8,128)(2,1)S(1)} %get-tuple-element.11.refs_1_, ...), custom_call_target="tpu_custom_call" | custom-call | tf_op jit(solution)/shard_map/pallas_call | solution.py:643

commit v3 on v2

--- a/solution.py
+++ b/solution.py
@@ -103,13 +103,7 @@
         return carry
 
     lax.fori_loop(0, B, build_spread, 0)
-    source = lax.broadcasted_iota(jnp.int32, (2 * N, N), 0)
-    for n, o in enumerate((0, 1, 3, 4)):
-        y = lax.broadcasted_iota(jnp.int32, (2 * N, N), 1) + (o - R)
-        y = jnp.where(y < 0, y + N + R, jnp.where(y >= N, y + C, y))
-        mover[:, n * N : (n + 1) * N] = jnp.where(source == y, 1.0, 0.0).astype(bf16)
     xpack[...] = jnp.zeros_like(xpack)
-    hpack[...] = jnp.zeros_like(hpack)
 
     def pack_edges(block, i, pack):
         first = jnp.zeros((C, N), bf16)
@@ -119,7 +113,7 @@
             first = jnp.where((lane >= 2 * x) & (lane < 2 * x + 2), turned, first)
             spot = (2 * x - 2) % N
             last = jnp.where((lane >= spot) & (lane < spot + 2), turned, last)
-        shift = 2 * CELL * lax.rem(i, 4)
+        shift = 2 * CELL * (i % 4)
         half = i // 4
         pack[0, half] = pack[0, half] + pltpu.roll(first, shift, 1)
         pack[1, half] = pack[1, half] + pltpu.roll(last, shift + 2, 1)
@@ -225,52 +219,20 @@
 
         return start, wait
 
-    coarse = (split_dot(pooled[...], spread[...], NT) / CELL).astype(bf16)
-    coarse_nb[4] = coarse
-    ones = jnp.where(lax.broadcasted_iota(jnp.int32, (8, N), 1) < C, 1.0, 0.0)
-
-    def as_row(values):
-        sums = dot(ones, values, NT, HIGHEST)
-        return jnp.concatenate([sums, jnp.zeros((8, N - C), f32)], axis=1)
-
-    top1[gy] = as_row(coarse.astype(f32)) / B
-
-    def widen(k, carry):
-        block = nw[k].astype(f32)
-        wide[k] = jnp.concatenate([block, block], axis=1)
-        turned = block.T
-        wide_t[k] = jnp.concatenate([turned, turned], axis=1)
-        return carry
-
-    lax.fori_loop(0, K, widen, 0, unroll=4)
-
-    code = (offs[pl.ds(0, 1), :] + R) * W + offs[pl.ds(1, 1), :] + R
-
-    def coded(points, stride, first):
-        row = lax.broadcasted_iota(jnp.int32, (points, K), 0) * stride + first
-        col = lax.broadcasted_iota(jnp.int32, (points, K), 1)
-        hit = jnp.where(row == col, jnp.broadcast_to(code, (points, K)).astype(f32), 0.0)
-        own = jnp.sum(hit, axis=1, keepdims=True).astype(jnp.int32)
-        return jnp.broadcast_to(own, (points, N))
-
-    codes[...] = coded(K, 1, 0)
-
-    def place(p, carry):
-        plain = jnp.zeros((C, N), f32)
-        turned = jnp.zeros((C, N), f32)
-        for k in range(K):
-            mine = codes[pl.ds(k, 1), :] == p
-            plain = plain + jnp.where(mine, wide[k], 0.0)
-            turned = turned + jnp.where(mine, wide_t[k], 0.0)
-        w5[p] = plain.astype(bf16)
-        w5t[p] = turned.astype(bf16)
-        return carry
-
-    lax.fori_loop(0, W * W, place, 0, unroll=5)
     pl.semaphore_wait(barrier, nx - 1 + ny - 1 + 4)
     xhalo = halo_copies(xs, xpack, xright, xleft, halo_s, halo_r)
     for copy in xhalo:
         copy.start()
+
+    coarse = (split_dot(pooled[...], spread[...], NT) / CELL).astype(bf16)
+    coarse_nb[4] = coarse
+    ones = jnp.where(lax.broadcasted_iota(jnp.int32, (8, N), 1) < C, 1.0, 0.0)
+
+    def as_row(values):
+        sums = dot(ones, values, NT, HIGHEST)
+        return jnp.concatenate([sums, jnp.zeros((8, N - C), f32)], axis=1)
+
+    top1[gy] = as_row(coarse.astype(f32)) / B
 
     coarse_copies = []
     for n, (dx, dy) in enumerate(around()):
@@ -284,6 +246,44 @@
     t1_start, t1_wait = line("gy", lambda p: top1.at[gy], lambda p: top1.at[p], t1_s, t1_r)
     t1_start()
 
+    hpack[...] = jnp.zeros_like(hpack)
+    source = lax.broadcasted_iota(jnp.int32, (2 * N, N), 0)
+    for n, o in enumerate((0, 1, 3, 4)):
+        y = lax.broadcasted_iota(jnp.int32, (2 * N, N), 1) + (o - R)
+        y = jnp.where(y < 0, y + N + R, jnp.where(y >= N, y + C, y))
+        mover[:, n * N : (n + 1) * N] = jnp.where(source == y, 1.0, 0.0).astype(bf16)
+    def widen(k, carry):
+        block = nw[k].astype(f32)
+        wide[k] = jnp.concatenate([block, block], axis=1)
+        turned = block.T
+        wide_t[k] = jnp.concatenate([turned, turned], axis=1)
+        return carry
+
+    lax.fori_loop(0, K, widen, 0, unroll=4)
+
+    code = (offs[pl.ds(0, 1), :] + R) * W + offs[pl.ds(1, 1), :] + R
+
+    def coded(points, stride, first):
+        row = lax.broadcasted_iota(jnp.int32, (points, K), 0) * stride + first
+        col = lax.broadcasted_iota(jnp.int32, (points, K), 1)
+        hit = jnp.where(row == col, jnp.broadcast_to(code, (points, K)).astype(f32), 0.0)
+        own = jnp.sum(hit, axis=1, keepdims=True).astype(jnp.int32)
+        return jnp.broadcast_to(own, (points, N))
+
+    codes[...] = coded(K, 1, 0)
+
+    def place(p, carry):
+        plain = jnp.zeros((C, N), f32)
+        turned = jnp.zeros((C, N), f32)
+        for k in range(K):
+            mine = codes[pl.ds(k, 1), :] == p
+            plain = plain + jnp.where(mine, wide[k], 0.0)
+            turned = turned + jnp.where(mine, wide_t[k], 0.0)
+        w5[p] = plain.astype(bf16)
+        w5t[p] = turned.astype(bf16)
+        return carry
+
+    lax.fori_loop(0, W * W, place, 0, unroll=5)
     nothing = jnp.zeros((C, N), bf16)
 
     def band(o, carry):
@@ -352,11 +352,11 @@
             parts.append(jnp.concatenate([first, second], axis=1))
         return dot(matrix[...], jnp.concatenate(parts, axis=0))
 
-    def near_field(pair, carry):
+    def near_field(pair):
         near_buf[pair] = banded(fwd, xs, pair)
-        return carry
-
-    lax.fori_loop(0, N // (2 * GROUP), near_field, 0, unroll=True)
+
+    for pair in range(B):
+        near_field(pair)
     t2_wait()
     me = gx * ny + gy
     top_all = top2[...].reshape(N, N)
@@ -369,11 +369,11 @@
 
     loads[1].wait()
 
-    def forward(i, carry):
-        rows16 = pl.ds(pl.multiple_of(i * CELL, CELL), CELL)
+    def forward(i):
+        rows16 = pl.ds(i * CELL, CELL)
         upstream = jnp.swapaxes(cbuf[:, rows16, :], 0, 1)
         shared = base[i]
-        actives, slopes = [], []
+        actives = []
         total = jnp.zeros((C, N), f32)
         for half in range(2):
             for g in range(2):
@@ -390,19 +390,28 @@
                     )
                     grad = (upstream[x].astype(f32) * slope).astype(bf16)
                     hs[R, R + i * CELL + x] = grad
-                    slopes.append(grad)
                     total = total + grad.astype(f32)
-        pooled[:, pl.ds(pl.multiple_of(i * N, N), N)] = total
-        pack_edges(slopes, i, hpack)
+        pooled[:, pl.ds(i * N, N)] = total
         active = jnp.swapaxes(jnp.stack(actives), 0, 1)
         obuf[:, rows16, :] = (fbuf[:, rows16, :].astype(f32) + active).astype(bf16)
-        return carry
-
-    lax.fori_loop(0, B, forward, 0)
-
-    hhalo = halo_copies(hs, hpack, hright, hleft, hhalo_s, hhalo_r)
-    for copy in hhalo:
-        copy.start()
+
+    def weigh(o, half):
+        groups = [half * (N // GROUP // 2) + i for i in range(N // GROUP // 2)]
+        left = jnp.concatenate(
+            [xs[o, pl.ds(i * GROUP, BAND)].reshape(BAND * C, N) for i in groups], axis=1
+        )
+        right = jnp.concatenate(
+            [hs[R, pl.ds(R + i * GROUP, GROUP)].reshape(GROUP * C, N) for i in groups], axis=1
+        )
+        return dot(left, right, NT)
+
+    for i in range(B // 2):
+        near_field(B + 2 * i)
+        near_field(B + 2 * i + 1)
+        forward(i)
+    for i in range(B // 2):
+        grads[i] = weigh(i, 0)
+        forward(B // 2 + i)
 
     one = split_dot(pooled[...], spread[...], NT)
     one_ref[...] = one
@@ -410,21 +419,8 @@
     u1_start, u1_wait = line("gy", lambda p: two1.at[gy], lambda p: two1.at[p], u1_s, u1_r)
     u1_start()
 
-    left = jnp.concatenate(
-        [
-            jnp.concatenate(
-                [xs[o, pl.ds(i * GROUP, BAND)].reshape(BAND * C, N) for i in range(N // GROUP)],
-                axis=1,
-            )
-            for o in range(W)
-        ],
-        axis=0,
-    )
-    right = jnp.concatenate(
-        [hs[R, pl.ds(R + i * GROUP, GROUP)].reshape(GROUP * C, N) for i in range(N // GROUP)],
-        axis=1,
-    )
-    grads[...] = dot(left, right, NT).reshape(W, BAND * C, GROUP * C)
+    for o in range(W):
+        grads[o] = weigh(o, 1) + (grads[o] if o < B // 2 else weigh(o, 0))
     u1_wait()
     two2[gx] = two1[:, 0, :]
     u2_start, u2_wait = line("gx", lambda p: two2.at[gx], lambda p: two2.at[p], u2_s, u2_r)
@@ -460,6 +456,15 @@
     rs1[gy] = rs_src[gy]
     r1_start, r1_wait = line("gy", lambda p: rs_src.at[p], lambda p: rs1.at[p], r1_s, r1_r)
     r1_start()
+
+    def pack_hidden(i, carry):
+        pack_edges(hs[R, pl.ds(R + i * CELL, CELL)], i, hpack)
+        return carry
+
+    lax.fori_loop(0, B, pack_hidden, 0)
+    hhalo = halo_copies(hs, hpack, hright, hleft, hhalo_s, hhalo_r)
+    for copy in hhalo:
+        copy.start()
 
     def push(l, total):
         grad = one_ref[...]
@@ -478,6 +483,14 @@
         )
         copy.start()
         push_copies.append(copy)
+
+    r1_wait()
+    total = rs1[0].astype(f32)
+    for j in range(1, ny):
+        total = total + rs1[j].astype(f32)
+    rs2[gx] = total.astype(bf16)
+    r2_start, r2_wait = line("gx", lambda p: rs2.at[gx], lambda p: rs2.at[p], r2_s, r2_r)
+    r2_start()
 
     for copy in hhalo:
         copy.wait()
@@ -521,15 +534,7 @@
         ibuf[:, rows16, :] = (cbuf[:, rows16, :].astype(f32) + total).astype(bf16)
         return carry
 
-    lax.fori_loop(0, 3, backward, 0, unroll=True)
-    r1_wait()
-    total = rs1[0].astype(f32)
-    for j in range(1, ny):
-        total = total + rs1[j].astype(f32)
-    rs2[gx] = total.astype(bf16)
-    r2_start, r2_wait = line("gx", lambda p: rs2.at[gx], lambda p: rs2.at[p], r2_s, r2_r)
-    r2_start()
-    lax.fori_loop(3, 6, backward, 0, unroll=True)
+    lax.fori_loop(0, 1, backward, 0, unroll=True)
     r2_wait()
     total = rs2[0].astype(f32)
     for j in range(1, nx):
@@ -537,7 +542,7 @@
     ag[gy] = total.astype(bf16)
     a1_start, a1_wait = line("gy", lambda p: ag.at[gy], lambda p: ag.at[p], a1_s, a1_r)
     a1_start()
-    lax.fori_loop(6, B, backward, 0, unroll=True)
+    lax.fori_loop(1, B, backward, 0, unroll=True)
     a1_wait()
     for k in range(K):
         whole = ag[k].astype(f32)

time: 70 us -> 62.1 us (0.89)
  Pallas kernels: 69 us -> 61.1 us
    pallas_call x1, Pallas kernels: 66.8 us -> 58.8 us  [per_device(): pl.pallas_call(functools.partial(kernel, nx, ny), out_shape=[pltpu.VMEM(*...]
where the time goes in v3:
time: 62.1 us; the launch traced here: 62 us
  Pallas kernels  61.1 us (98%)
  between operations  0.82 us (1%)
    pallas_call x1, Pallas kernels, per_device(): pl.pallas_call(functools.partial(kernel, nx, ny), out_shape=[pltpu.VMEM(*...  58.8 us
    pallas_call x1, Pallas kernels, per_device(): pl.pallas_call(store, out_shape=[jax.ShapeDtypeStruct(*result) for result...  2.29 us

profile of v3, /device:TPU:1, one launch (start us, length us, event | category | flops | bytes accessed | tf_op | source)
XLA Modules:
  0.0 62.0 jit_solution(17672212823664224)
XLA Ops:
  0.6 58.8 %shard_map.119 = (bf16[64,128,128]{2,1,0:T(8,128)(2,1)S(1)}, bf16[64,128,128]{2,1,0:T(8,128)(2,1)S(1)}, f32[16,64,64]{2,1,0:T(8,128)S(1)}, f32[8,64,64]{2,1,0:T(8,128)S(1)}, f32[64,64]{1,0:T(8,128)S(1)}) custom-call(bf16[64,128,128]{2,1,0:T(8,128)(2,1)} %feat.1, bf16[64,128,128]{2,1,0:T(8,128)(2,1)} %cot.1, s32[64,8,128]{2,1,0:T(8,128)} %bitcast.2, ...), custom_call_target="tpu_custom_call" | custom-call | tf_op jit(solution)/shard_map/pallas_call | solution.py:630
  59.5 2.3 %shard_map.120 = (bf16[64,128,128]{2,1,0:T(8,128)(2,1)}, bf16[64,128,128]{2,1,0:T(8,128)(2,1)}, f32[16,64,64]{2,1,0:T(8,128)}, f32[8,64,64]{2,1,0:T(8,128)}, f32[64,64]{1,0:T(8,128)}) custom-call(bf16[64,128,128]{2,1,0:T(8,128)(2,1)S(1)} %get-tuple-element.10.refs_0_, bf16[64,128,128]{2,1,0:T(8,128)(2,1)S(1)} %get-tuple-element.11.refs_1_, ...), custom_call_target="tpu_custom_call" | custom-call | tf_op jit(solution)/shard_map/pallas_call | solution.py:648

commit v4 on v3

--- a/solution.py
+++ b/solution.py
@@ -59,9 +59,9 @@
 
 def kernel(
     nx, ny,
-    feat, cot, adj, offs, spots, nw, lw, tw, tk,
+    feat, cot, adj, offs_in, spots, nw_in, lw_in, tw_in, tk_in,
     obuf, ibuf, near_out, link_out, top_out,
-    fbuf, cbuf, abuf, xs, hs, xpack, hpack, xright, xleft, hright, hleft,
+    fbuf, cbuf, abuf, offs, nw, lw, tw, tk, xs, hs, xpack, hpack, xright, xleft, hright, hleft,
     wide, wide_t, w5, w5t, fwd, bwd, spread, pooled, onehot, idx,
     coarse_nb, picked, base, top1, top2, two1, two2, ctr, rctr, grads,
     rs_src, rs1, rs2, ag, one_ref, codes, mover, edges, near_buf, stencil,
@@ -75,10 +75,22 @@
     def at(dx, dy):
         return (lax.rem(gx + dx + nx, nx), lax.rem(gy + dy + ny, ny))
 
-    loads = [
-        pltpu.make_async_copy(feat, fbuf, load_sem.at[0]),
-        pltpu.make_async_copy(cot, cbuf, load_sem.at[1]),
-        pltpu.make_async_copy(adj.at[pl.ds(gx * B, B)], abuf, load_sem.at[2]),
+    quarter = N // 4
+    field_loads = [
+        pltpu.make_async_copy(
+            feat.at[:, pl.ds(n * quarter, quarter), :], fbuf.at[:, pl.ds(n * quarter, quarter), :],
+            load_sem.at[n],
+        )
+        for n in range(4)
+    ]
+    loads = field_loads + [
+        pltpu.make_async_copy(source, target, load_sem.at[4 + n])
+        for n, (source, target) in enumerate(
+            (
+                (offs_in, offs), (nw_in, nw), (adj.at[pl.ds(gx * B, B)], abuf), (lw_in, lw),
+                (tw_in, tw), (tk_in, tk), (cot, cbuf),
+            )
+        )
     ]
     for load in loads:
         load.start()
@@ -118,7 +130,6 @@
         pack[0, half] = pack[0, half] + pltpu.roll(first, shift, 1)
         pack[1, half] = pack[1, half] + pltpu.roll(last, shift + 2, 1)
 
-    loads[0].wait()
 
     def arrange(i, carry):
         block = jnp.swapaxes(fbuf[:, pl.ds(pl.multiple_of(i * CELL, CELL), CELL), :], 0, 1)
@@ -130,7 +141,9 @@
         pack_edges(block, i, xpack)
         return carry
 
-    lax.fori_loop(0, B, arrange, 0)
+    for n in range(4):
+        field_loads[n].wait()
+        lax.fori_loop(2 * n, 2 * n + 2, arrange, 0)
 
     def halo_copies(field, pack, right, left, send, recv):
         mid = field.at[R]
@@ -252,6 +265,8 @@
         y = lax.broadcasted_iota(jnp.int32, (2 * N, N), 1) + (o - R)
         y = jnp.where(y < 0, y + N + R, jnp.where(y >= N, y + C, y))
         mover[:, n * N : (n + 1) * N] = jnp.where(source == y, 1.0, 0.0).astype(bf16)
+    for load in loads[4:]:
+        load.wait()
     def widen(k, carry):
         block = nw[k].astype(f32)
         wide[k] = jnp.concatenate([block, block], axis=1)
@@ -302,7 +317,6 @@
 
     lax.fori_loop(0, W, band, 0, unroll=True)
 
-    loads[2].wait()
     lane8 = lax.broadcasted_iota(jnp.int32, (L, N), 1)
     found = jnp.zeros((L, N), jnp.int32)
     for i in range(B):
@@ -367,7 +381,6 @@
     for i in range(B):
         base[i] = spread_one[:, i * N : (i + 1) * N]
 
-    loads[1].wait()
 
     def forward(i):
         rows16 = pl.ds(i * CELL, CELL)
@@ -555,9 +568,17 @@
 def store(*refs):
     count = len(refs) // 2
     sems = refs[-1]
-    copies = [
-        pltpu.make_async_copy(refs[n], refs[count + n], sems.at[n]) for n in range(count)
-    ]
+    copies = []
+    for n in range(count):
+        pieces = 4 if n < 2 else 1
+        size = refs[n].shape[0] // pieces
+        for piece in range(pieces):
+            rows = pl.ds(piece * size, size)
+            copies.append(
+                pltpu.make_async_copy(
+                    refs[n].at[rows], refs[count + n].at[rows], sems.at[len(copies)]
+                )
+            )
     for copy in copies:
         copy.start()
     for copy in copies:
@@ -575,6 +596,11 @@
             pltpu.VMEM((C, N, N), bf16),
             pltpu.VMEM((C, N, N), bf16),
             pltpu.VMEM((B, L, N), jnp.int32),
+            pltpu.VMEM((2, K), jnp.int32),
+            pltpu.VMEM((K, C, C), bf16),
+            pltpu.VMEM((L, C, C), bf16),
+            pltpu.VMEM((C, C), bf16),
+            pltpu.VMEM((N, N), f32),
             pltpu.VMEM((W, HALO, C, N), bf16),
             pltpu.VMEM((W, HALO, C, N), bf16),
             pltpu.VMEM((2, 2, C, N), bf16),
@@ -613,7 +639,7 @@
             pltpu.VMEM((8, C, N), bf16),
             pltpu.VMEM((N // (2 * GROUP), GROUP * C, 2 * N), f32),
             pltpu.VMEM((W * W, 32, N), f32),
-            dma((3,)),
+            dma((11,)),
             dma((8,)), dma((8,)), dma((8,)), dma((8,)),
             dma((8,)), dma((8,)), dma((8,)), dma((8,)),
             dma((ny,)), dma((ny,)), dma((nx,)), dma((nx,)),
@@ -631,10 +657,9 @@
             functools.partial(kernel, nx, ny),
             out_shape=[pltpu.VMEM(*result) for result in results],
             in_specs=[
-                anywhere, anywhere, anywhere,
-                vmem,
+                anywhere, anywhere, anywhere, anywhere,
                 pl.BlockSpec(memory_space=pltpu.SMEM),
-                vmem, vmem, vmem, vmem,
+                anywhere, anywhere, anywhere, anywhere,
             ],
             out_specs=[vmem] * 5,
             scratch_shapes=scratch,
@@ -650,7 +675,7 @@
             out_shape=[jax.ShapeDtypeStruct(*result) for result in results],
             in_specs=[vmem] * 5,
             out_specs=[anywhere] * 5,
-            scratch_shapes=[dma((5,))],
+            scratch_shapes=[dma((11,))],
             compiler_params=pltpu.CompilerParams(vmem_limit_bytes=2**20),
         )(*[pltpu.with_memory_space_constraint(value, pltpu.VMEM) for value in held])
 

time: 62.1 us -> 59.6 us (0.960)
  Pallas kernels: 61.1 us -> 58.7 us
    pallas_call x1, Pallas kernels: 58.8 us -> 56.3 us  [per_device(): pl.pallas_call(functools.partial(kernel, nx, ny), out_shape=[pltpu.VMEM(*...]
where the time goes in v4:
time: 59.6 us; the launch traced here: 59.5 us
  Pallas kernels  58.7 us (98%)
  between operations  0.82 us (1%)
    pallas_call x1, Pallas kernels, per_device(): pl.pallas_call(functools.partial(kernel, nx, ny), out_shape=[pltpu.VMEM(*...  56.3 us
    pallas_call x1, Pallas kernels, per_device(): pl.pallas_call(store, out_shape=[jax.ShapeDtypeStruct(*result) for result...  2.34 us

profile of v4, /device:TPU:1, one launch (start us, length us, event | category | flops | bytes accessed | tf_op | source)
XLA Modules:
  0.0 59.5 jit_solution(10400574618247491253)
XLA Ops:
  0.6 56.3 %shard_map.119 = (bf16[64,128,128]{2,1,0:T(8,128)(2,1)S(1)}, bf16[64,128,128]{2,1,0:T(8,128)(2,1)S(1)}, f32[16,64,64]{2,1,0:T(8,128)S(1)}, f32[8,64,64]{2,1,0:T(8,128)S(1)}, f32[64,64]{1,0:T(8,128)S(1)}) custom-call(bf16[64,128,128]{2,1,0:T(8,128)(2,1)} %feat.1, bf16[64,128,128]{2,1,0:T(8,128)(2,1)} %cot.1, s32[64,8,128]{2,1,0:T(8,128)} %bitcast.2, ...), custom_call_target="tpu_custom_call" | custom-call | tf_op jit(solution)/shard_map/pallas_call | solution.py:656
  57.0 2.3 %shard_map.120 = (bf16[64,128,128]{2,1,0:T(8,128)(2,1)}, bf16[64,128,128]{2,1,0:T(8,128)(2,1)}, f32[16,64,64]{2,1,0:T(8,128)}, f32[8,64,64]{2,1,0:T(8,128)}, f32[64,64]{1,0:T(8,128)}) custom-call(bf16[64,128,128]{2,1,0:T(8,128)(2,1)S(1)} %get-tuple-element.10.refs_0_, bf16[64,128,128]{2,1,0:T(8,128)(2,1)S(1)} %get-tuple-element.11.refs_1_, ...), custom_call_target="tpu_custom_call" | custom-call | tf_op jit(solution)/shard_map/pallas_call | solution.py:673

commit v5 on v4

--- a/solution.py
+++ b/solution.py
@@ -357,7 +357,6 @@
         turned = lw[l].astype(f32).T.astype(bf16)
         return total + dot(turned, chosen)
 
-    level_one = lax.fori_loop(0, L, pick, jnp.zeros((C, N), f32), unroll=True)
     def banded(matrix, field, pair):
         parts = []
         for o in range(W):
@@ -369,7 +368,10 @@
     def near_field(pair):
         near_buf[pair] = banded(fwd, xs, pair)
 
-    for pair in range(B):
+    for pair in range(B // 2):
+        near_field(pair)
+    level_one = lax.fori_loop(0, L, pick, jnp.zeros((C, N), f32), unroll=True)
+    for pair in range(B // 2, B):
         near_field(pair)
     t2_wait()
     me = gx * ny + gy
@@ -397,7 +399,8 @@
                     square = v * v
                     tangent = jnp.tanh(v * (root_scale + root_scale * cubic_term * square))
                     gate = 0.5 + 0.5 * tangent
-                    actives.append(v * gate)
+                    own = xs[R, R + i * CELL + x].astype(f32)
+                    actives.append((own + v * gate).astype(bf16))
                     slope = gate + v * (gate - gate * gate) * (
                         2.0 * root_scale + 6.0 * root_scale * cubic_term * square
                     )
@@ -405,8 +408,7 @@
                     hs[R, R + i * CELL + x] = grad
                     total = total + grad.astype(f32)
         pooled[:, pl.ds(i * N, N)] = total
-        active = jnp.swapaxes(jnp.stack(actives), 0, 1)
-        obuf[:, rows16, :] = (fbuf[:, rows16, :].astype(f32) + active).astype(bf16)
+        obuf[:, rows16, :] = jnp.swapaxes(jnp.stack(actives), 0, 1)
 
     def weigh(o, half):
         groups = [half * (N // GROUP // 2) + i for i in range(N // GROUP // 2)]
@@ -428,17 +430,8 @@
 
     one = split_dot(pooled[...], spread[...], NT)
     one_ref[...] = one
-    two1[gy] = as_row(one)
-    u1_start, u1_wait = line("gy", lambda p: two1.at[gy], lambda p: two1.at[p], u1_s, u1_r)
-    u1_start()
-
     for o in range(W):
         grads[o] = weigh(o, 1) + (grads[o] if o < B // 2 else weigh(o, 0))
-    u1_wait()
-    two2[gx] = two1[:, 0, :]
-    u2_start, u2_wait = line("gx", lambda p: two2.at[gx], lambda p: two2.at[p], u2_s, u2_r)
-    u2_start()
-
     def stencil_grad(p, carry):
         a = p // W
         b = lax.rem(p, W)
@@ -469,6 +462,9 @@
     rs1[gy] = rs_src[gy]
     r1_start, r1_wait = line("gy", lambda p: rs_src.at[p], lambda p: rs1.at[p], r1_s, r1_r)
     r1_start()
+    two1[gy] = as_row(one_ref[...])
+    u1_start, u1_wait = line("gy", lambda p: two1.at[gy], lambda p: two1.at[p], u1_s, u1_r)
+    u1_start()
 
     def pack_hidden(i, carry):
         pack_edges(hs[R, pl.ds(R + i * CELL, CELL)], i, hpack)
@@ -504,6 +500,10 @@
     rs2[gx] = total.astype(bf16)
     r2_start, r2_wait = line("gx", lambda p: rs2.at[gx], lambda p: rs2.at[p], r2_s, r2_r)
     r2_start()
+    u1_wait()
+    two2[gx] = two1[:, 0, :]
+    u2_start, u2_wait = line("gx", lambda p: two2.at[gx], lambda p: two2.at[p], u2_s, u2_r)
+    u2_start()
 
     for copy in hhalo:
         copy.wait()
@@ -521,6 +521,13 @@
         else:
             odds = odds + rctr[slot]
     collected = evens + pltpu.roll(odds, C, 1)
+    r2_wait()
+    total = rs2[0].astype(f32)
+    for j in range(1, nx):
+        total = total + rs2[j].astype(f32)
+    ag[gy] = total.astype(bf16)
+    a1_start, a1_wait = line("gy", lambda p: ag.at[gy], lambda p: ag.at[p], a1_s, a1_r)
+    a1_start()
     u2_wait()
     two_all = two2[...].reshape(N, N)[:, :C]
     kernel_grad = dot(tk[...], two_all, TN, HIGHEST)
@@ -547,15 +554,7 @@
         ibuf[:, rows16, :] = (cbuf[:, rows16, :].astype(f32) + total).astype(bf16)
         return carry
 
-    lax.fori_loop(0, 1, backward, 0, unroll=True)
-    r2_wait()
-    total = rs2[0].astype(f32)
-    for j in range(1, nx):
-        total = total + rs2[j].astype(f32)
-    ag[gy] = total.astype(bf16)
-    a1_start, a1_wait = line("gy", lambda p: ag.at[gy], lambda p: ag.at[p], a1_s, a1_r)
-    a1_start()
-    lax.fori_loop(1, B, backward, 0, unroll=True)
+    lax.fori_loop(0, B, backward, 0, unroll=True)
     a1_wait()
     for k in range(K):
         whole = ag[k].astype(f32)

time: 59.6 us -> 58.4 us (0.980)
  Pallas kernels: 58.7 us -> 57.5 us
    pallas_call x1, Pallas kernels: 56.3 us -> 55.1 us  [per_device(): pl.pallas_call(functools.partial(kernel, nx, ny), out_shape=[pltpu.VMEM(*...]
where the time goes in v5:
time: 58.4 us; the launch traced here: 58.3 us
  Pallas kernels  57.5 us (98%)
  between operations  0.82 us (1%)
    pallas_call x1, Pallas kernels, per_device(): pl.pallas_call(functools.partial(kernel, nx, ny), out_shape=[pltpu.VMEM(*...  55.1 us
    pallas_call x1, Pallas kernels, per_device(): pl.pallas_call(store, out_shape=[jax.ShapeDtypeStruct(*result) for result...  2.34 us

profile of v5, /device:TPU:1, one launch (start us, length us, event | category | flops | bytes accessed | tf_op | source)
XLA Modules:
  0.0 58.3 jit_solution(17589601719863848804)
XLA Ops:
  0.6 55.1 %shard_map.119 = (bf16[64,128,128]{2,1,0:T(8,128)(2,1)S(1)}, bf16[64,128,128]{2,1,0:T(8,128)(2,1)S(1)}, f32[16,64,64]{2,1,0:T(8,128)S(1)}, f32[8,64,64]{2,1,0:T(8,128)S(1)}, f32[64,64]{1,0:T(8,128)S(1)}) custom-call(bf16[64,128,128]{2,1,0:T(8,128)(2,1)} %feat.1, bf16[64,128,128]{2,1,0:T(8,128)(2,1)} %cot.1, s32[64,8,128]{2,1,0:T(8,128)} %bitcast.2, ...), custom_call_target="tpu_custom_call" | custom-call | tf_op jit(solution)/shard_map/pallas_call | solution.py:655
  55.8 2.3 %shard_map.120 = (bf16[64,128,128]{2,1,0:T(8,128)(2,1)}, bf16[64,128,128]{2,1,0:T(8,128)(2,1)}, f32[16,64,64]{2,1,0:T(8,128)}, f32[8,64,64]{2,1,0:T(8,128)}, f32[64,64]{1,0:T(8,128)}) custom-call(bf16[64,128,128]{2,1,0:T(8,128)(2,1)S(1)} %get-tuple-element.10.refs_0_, bf16[64,128,128]{2,1,0:T(8,128)(2,1)S(1)} %get-tuple-element.11.refs_1_, ...), custom_call_target="tpu_custom_call" | custom-call | tf_op jit(solution)/shard_map/pallas_call | solution.py:672

commit v6 on v5

--- a/solution.py
+++ b/solution.py
@@ -432,6 +432,8 @@
     one_ref[...] = one
     for o in range(W):
         grads[o] = weigh(o, 1) + (grads[o] if o < B // 2 else weigh(o, 0))
+        for i in range(2 * o, min(2 * o + 2, B)):
+            pack_edges(hs[R, pl.ds(R + i * CELL, CELL)], i, hpack)
     def stencil_grad(p, carry):
         a = p // W
         b = lax.rem(p, W)
@@ -462,18 +464,12 @@
     rs1[gy] = rs_src[gy]
     r1_start, r1_wait = line("gy", lambda p: rs_src.at[p], lambda p: rs1.at[p], r1_s, r1_r)
     r1_start()
+    hhalo = halo_copies(hs, hpack, hright, hleft, hhalo_s, hhalo_r)
+    for copy in hhalo:
+        copy.start()
     two1[gy] = as_row(one_ref[...])
     u1_start, u1_wait = line("gy", lambda p: two1.at[gy], lambda p: two1.at[p], u1_s, u1_r)
     u1_start()
-
-    def pack_hidden(i, carry):
-        pack_edges(hs[R, pl.ds(R + i * CELL, CELL)], i, hpack)
-        return carry
-
-    lax.fori_loop(0, B, pack_hidden, 0)
-    hhalo = halo_copies(hs, hpack, hright, hleft, hhalo_s, hhalo_r)
-    for copy in hhalo:
-        copy.start()
 
     def push(l, total):
         grad = one_ref[...]

time: 58.4 us -> 62.7 us (1.074)
  Pallas kernels: 57.5 us -> 61.8 us
    pallas_call x1, Pallas kernels: 55.1 us -> 59.4 us  [per_device(): pl.pallas_call(functools.partial(kernel, nx, ny), out_shape=[pltpu.VMEM(*...]
where the time goes in v6:
time: 62.7 us; the launch traced here: 62.6 us
  Pallas kernels  61.8 us (99%)
  between operations  0.82 us (1%)
    pallas_call x1, Pallas kernels, per_device(): pl.pallas_call(functools.partial(kernel, nx, ny), out_shape=[pltpu.VMEM(*...  59.4 us
    pallas_call x1, Pallas kernels, per_device(): pl.pallas_call(store, out_shape=[jax.ShapeDtypeStruct(*result) for result...  2.34 us

profile of v6, /device:TPU:1, one launch (start us, length us, event | category | flops | bytes accessed | tf_op | source)
XLA Modules:
  0.0 62.6 jit_solution(3581260273167470996)
XLA Ops:
  0.6 59.4 %shard_map.119 = (bf16[64,128,128]{2,1,0:T(8,128)(2,1)S(1)}, bf16[64,128,128]{2,1,0:T(8,128)(2,1)S(1)}, f32[16,64,64]{2,1,0:T(8,128)S(1)}, f32[8,64,64]{2,1,0:T(8,128)S(1)}, f32[64,64]{1,0:T(8,128)S(1)}) custom-call(bf16[64,128,128]{2,1,0:T(8,128)(2,1)} %feat.1, bf16[64,128,128]{2,1,0:T(8,128)(2,1)} %cot.1, s32[64,8,128]{2,1,0:T(8,128)} %bitcast.2, ...), custom_call_target="tpu_custom_call" | custom-call | tf_op jit(solution)/shard_map/pallas_call | solution.py:651
  60.1 2.3 %shard_map.120 = (bf16[64,128,128]{2,1,0:T(8,128)(2,1)}, bf16[64,128,128]{2,1,0:T(8,128)(2,1)}, f32[16,64,64]{2,1,0:T(8,128)}, f32[8,64,64]{2,1,0:T(8,128)}, f32[64,64]{1,0:T(8,128)}) custom-call(bf16[64,128,128]{2,1,0:T(8,128)(2,1)S(1)} %get-tuple-element.10.refs_0_, bf16[64,128,128]{2,1,0:T(8,128)(2,1)S(1)} %get-tuple-element.11.refs_1_, ...), custom_call_target="tpu_custom_call" | custom-call | tf_op jit(solution)/shard_map/pallas_call | solution.py:668
